TPU v7x, 32 devices: a whole 2x2x4 slice. The times are simulated.
32 devices in a mesh: head: 2 (over x), wide: 16 (over z, y, core).
Axes of the slice: x: 2, y: 2, z: 4, core: 2. Of those that a mesh axis runs over, the one named last changes fastest.
Arguments:
- queries: bfloat16 [4096, 2048], P('wide', 'head'), may hold values from -120 to 120
- keys: bfloat16 [4096, 2048], P('wide', 'head'), may hold values from -6 to 6
- values: bfloat16 [4096, 2048], P('wide', 'head'), may hold values from -6 to 6
- out_grad: bfloat16 [4096, 2048], P('wide', 'head'), may hold values from -6 to 6
- qkv_weight: bfloat16 [3, 4096, 2048], P(None, 'wide', 'head'), may hold values from -0.125 to 0.125
- doc_lengths: int32 [8], replicated, may hold values from 1 to 1023, as said below
- image_count: int32 [16], replicated, may hold values 0 or 1
- image_offset: int32 [16], replicated, may hold values from 0 to 192
- slab_owner: int32 [16], replicated, may hold values from 0 to 15, each once
- patch_weight: bfloat16 [256, 4096], P(None, 'head'), may hold values from -0.09375 to 0.09375
- conv_input: bfloat16 [16, 8, 8, 128], P('wide', 'head'), may hold values from -20 to 20
- pre_act: bfloat16 [16, 8, 8, 128], P('wide', 'head'), may hold values from -6 to 6
- kernel_first: float32 [1152, 128], P('wide'), may hold values from -0.1875 to 0.1875
- kernel_second: float32 [1152, 256], P('wide'), may hold values from -0.1875 to 0.1875
- mean_first: float32 [1152, 128], P('wide'), may hold values from -4 to 4
- mean_second: float32 [1152, 256], P('wide'), may hold values from -4 to 4
- square_first: float32 [1152, 128], P('wide'), may hold values from 0.05 to 1
- square_second: float32 [1152, 256], P('wide'), may hold values from 0.05 to 1
Outputs:
- input_grad_t: bfloat16 [4096, 4096], P('head', 'wide')
- new_kernel_first: float32 [1152, 128], P('wide')
- new_kernel_second: float32 [1152, 256], P('wide')
- new_mean_first: float32 [1152, 128], P('wide')
- new_mean_second: float32 [1152, 256], P('wide')
- new_square_first: float32 [1152, 128], P('wide')
- new_square_second: float32 [1152, 256], P('wide')
Inputs may be any that keep to these rules, and one draw needn't show every extreme that they name: `doc_lengths`: the first document is longer than 256 and shorter than 768; the last has 1024 minus the first one's length; the documents between come in consecutive pairs whose lengths add up to 1024.
All inputs are finite; a program needn't handle non-finite values.
Results may differ from a plain program's by a relative error of at most 0.013.
Values may be sent and summed in bfloat16 or wider, within the bound.
A program may use at most 128 MiB of HBM per device.

v0:
```python
import math

import jax
import jax.numpy as jnp
from jax import lax
from jax.sharding import PartitionSpec as P

HD = 128
REACH = 4
PROWS = 8
PCOLS = 8
PCH = 256
CMID = 128
CIN = 128
IMGTOK = 64


neg_big = -1e30
beta_one = 0.9
beta_two = 0.95
adam_eps = 1e-08
learn_rate = 0.02
decay_rate = 0.1
adam_step = 10
norm_eps = 1e-06


def passed_along(block, axis, distance):
    devices = range(lax.axis_size(axis))
    route = [(i - distance, i) for i in devices if i - distance in devices]
    return lax.ppermute(block, axis, route)


def with_halo(cells, sides, width):
    for axis, dim in sides:
        count = lax.axis_size(axis)
        ends = count - 1
        head = lax.slice_in_dim(cells, 0, width, axis=dim)
        tail = lax.slice_in_dim(cells, cells.shape[dim] - width, cells.shape[dim], axis=dim)
        cells = jnp.concatenate(
            [
                lax.ppermute(tail, axis, [(i, (i + 1) % count) for i in range(ends)]),
                cells,
                lax.ppermute(head, axis, [((i + 1) % count, i) for i in range(ends)]),
            ],
            axis=dim,
        )
    return cells


def pick_entry(lookup, wanted):
    return jnp.sum(jnp.where(jnp.arange(lookup.shape[0]) == wanted, lookup, 0))


def doc_number(places, doc_lengths):
    ends = jnp.cumsum(doc_lengths)
    return jnp.sum((places[:, None] >= ends[None, :]).astype(jnp.int32), axis=1)


def image_number(block, local, image_count, image_offset):
    present = pick_entry(image_count, block)
    start = pick_entry(image_offset, block)
    inside = (present > 0) & (local >= start) & (local < start + IMGTOK)
    return jnp.where(inside, block, -1)


def allowed_mask(query_places, query_docs, query_images, key_places, key_docs, key_images):
    same_doc = query_docs[:, None] == key_docs[None, :]
    earlier = key_places[None, :] <= query_places[:, None]
    same_image = (query_images[:, None] == key_images[None, :]) & (query_images[:, None] >= 0)
    return same_doc & (earlier | same_image)


def attend_block(query, key_all, value_all, grad_out, allowed):
    scale = 1.0 / math.sqrt(HD)
    rows = query.shape[0]
    count = key_all.shape[0]
    query_h = query.reshape(rows, -1, HD)
    key_h = key_all.reshape(count, -1, HD)
    value_h = value_all.reshape(count, -1, HD)
    grad_h = grad_out.reshape(rows, -1, HD)
    scores = jnp.einsum("qhd,khd->hqk", query_h, key_h, preferred_element_type=jnp.float32) * scale
    scores = jnp.where(allowed[None], scores, neg_big)
    top = jnp.max(scores, axis=-1, keepdims=True)
    expo = jnp.where(allowed[None], jnp.exp(scores - top), 0.0)
    prob = expo / jnp.sum(expo, axis=-1, keepdims=True)
    prob_low = prob.astype(jnp.bfloat16)
    output = jnp.einsum("hqk,khd->qhd", prob_low, value_h, preferred_element_type=jnp.float32)
    delta = jnp.einsum("qhd,qhd->hq", grad_h.astype(jnp.float32), output)
    dprob = jnp.einsum("qhd,khd->hqk", grad_h, value_h, preferred_element_type=jnp.float32)
    dscore = (prob * (dprob - delta[:, :, None])).astype(jnp.bfloat16)
    dquery = jnp.einsum("hqk,khd->qhd", dscore, key_h, preferred_element_type=jnp.float32) * scale
    dkey = jnp.einsum("hqk,qhd->khd", dscore, query_h, preferred_element_type=jnp.float32) * scale
    dvalue = jnp.einsum("hqk,qhd->khd", prob_low, grad_h, preferred_element_type=jnp.float32)
    return (dquery.reshape(rows, -1), dkey.reshape(count, -1), dvalue.reshape(count, -1))


def adam_update(param, mean, square, grad):
    new_mean = beta_one * mean + (1.0 - beta_one) * grad
    new_square = beta_two * square + (1.0 - beta_two) * grad * grad
    fixed_mean = new_mean / (1.0 - beta_one**adam_step)
    fixed_square = new_square / (1.0 - beta_two**adam_step)
    new_param = param - learn_rate * (
        fixed_mean / (jnp.sqrt(fixed_square) + adam_eps) + decay_rate * param
    )
    return (new_param, new_mean, new_square)


def shards(
    queries,
    keys,
    values,
    out_grad,
    qkv_weight,
    doc_lengths,
    image_count,
    image_offset,
    slab_owner,
    patch_weight,
    conv_input,
    pre_act,
    kernel_first,
    kernel_second,
    mean_first,
    mean_second,
    square_first,
    square_second,
):
    tokens_here = queries.shape[0]
    wide_count = lax.axis_size("wide")
    head_count = lax.axis_size("head")
    device_index = lax.axis_index("wide")
    head_index = lax.axis_index("head")
    local_places = jnp.arange(tokens_here, dtype=jnp.int32)
    query_places = device_index * tokens_here + local_places
    query_docs = doc_number(query_places, doc_lengths)
    query_images = image_number(device_index, local_places, image_count, image_offset)
    own_block = jnp.stack([keys, values])
    blocks = [own_block]
    moving = own_block
    for offset in range(REACH):
        moving = passed_along(moving, "wide", 1)
        blocks.append(moving)
    masks = []
    for offset in range(REACH + 1):
        source = (device_index - offset) % wide_count
        key_places = source * tokens_here + local_places
        key_docs = doc_number(key_places, doc_lengths)
        key_images = image_number(source, local_places, image_count, image_offset)
        visible = allowed_mask(
            query_places, query_docs, query_images, key_places, key_docs, key_images
        )
        masks.append(visible & (device_index - offset >= 0))
    allowed = jnp.concatenate(masks, axis=1)
    key_all = jnp.concatenate([block[0] for block in blocks], axis=0)
    value_all = jnp.concatenate([block[1] for block in blocks], axis=0)
    dquery, dkey, dvalue = attend_block(queries, key_all, value_all, out_grad, allowed)
    parts = [
        jnp.stack(
            [
                dkey[offset * tokens_here : (offset + 1) * tokens_here],
                dvalue[offset * tokens_here : (offset + 1) * tokens_here],
            ]
        )
        for offset in range(REACH + 1)
    ]
    carried = jnp.zeros_like(parts[0])
    for offset in range(REACH):
        carried = passed_along(carried + parts[REACH - offset], "wide", -1)
    key_grads = parts[0] + carried
    grads = jnp.stack(
        [
            dquery.astype(jnp.bfloat16),
            key_grads[0].astype(jnp.bfloat16),
            key_grads[1].astype(jnp.bfloat16),
        ]
    )
    partial_value = jnp.einsum(
        "prk,ptk->rt",
        lax.all_gather(qkv_weight, "wide", axis=1, tiled=True),
        grads,
        preferred_element_type=jnp.float32,
    ).astype(jnp.bfloat16)
    input_grad_t = (
        lax.psum_scatter(partial_value, "head", scatter_dimension=0, tiled=True)
        .astype(jnp.float32)
        .astype(jnp.bfloat16)
    )
    patch_part = lax.dot_general(
        input_grad_t, patch_weight, (((0,), (1,)), ((), ())), preferred_element_type=jnp.float32
    )
    patch_grad = lax.psum(patch_part.astype(jnp.bfloat16), "head")
    slab_rows = PROWS // head_count
    has_image = pick_entry(image_count, device_index)
    offset_here = pick_entry(image_offset, device_index)
    segment = lax.dynamic_slice_in_dim(
        patch_grad, offset_here + head_index * slab_rows * PCOLS, slab_rows * PCOLS, 0
    ) * has_image.astype(jnp.bfloat16)
    chooser = (slab_owner == device_index).astype(jnp.bfloat16)
    target = pick_entry(slab_owner, device_index)
    outgoing = jnp.where(
        (jnp.arange(wide_count) == target)[:, None, None],
        segment[None],
        jnp.zeros_like(segment)[None],
    )
    arrived = lax.all_to_all(outgoing, "wide", split_axis=0, concat_axis=0, tiled=True)
    incoming = jnp.einsum("n,npc->pc", chooser, arrived, preferred_element_type=jnp.float32).astype(
        jnp.bfloat16
    )
    kernel_low = lax.all_gather(
        kernel_second.astype(jnp.bfloat16), "wide", axis=0, tiled=True
    ).reshape(CMID, 9, PCH)
    act = jax.nn.silu(pre_act.astype(jnp.float32)).astype(jnp.bfloat16)
    both = jnp.stack([conv_input, act])
    rims = with_halo(both, (("head", 2),), 1)
    rims = jnp.pad(rims, ((0, 0), (0, 0), (0, 0), (1, 1), (0, 0)))
    input_pad = rims[0]
    act_pad = rims[1]
    grad_img = incoming.reshape(1, slab_rows, PCOLS, PCH)
    grad_pad = with_halo(grad_img, (("head", 1),), 1)
    grad_pad = jnp.pad(grad_pad, ((0, 0), (0, 0), (1, 1), (0, 0)))
    second_list = []
    dact = jnp.zeros((slab_rows * PCOLS, CMID), jnp.float32)
    for row_shift in range(3):
        for col_shift in range(3):
            offset = row_shift * 3 + col_shift
            piece = act_pad[
                :, row_shift : row_shift + slab_rows, col_shift : col_shift + PCOLS
            ].reshape(-1, CMID)
            second_list.append(
                lax.dot_general(
                    piece, incoming, (((0,), (0,)), ((), ())), preferred_element_type=jnp.float32
                )
            )
            moved = grad_pad[
                :, 2 - row_shift : 2 - row_shift + slab_rows, 2 - col_shift : 2 - col_shift + PCOLS
            ].reshape(-1, PCH)
            dact = dact + lax.dot_general(
                moved,
                kernel_low[:, offset],
                (((1,), (1,)), ((), ())),
                preferred_element_type=jnp.float32,
            )
    grad_second = jnp.stack(second_list, axis=1).reshape(-1, PCH)
    pre_flat = pre_act.astype(jnp.float32).reshape(-1, CMID)
    sig = jax.nn.sigmoid(pre_flat)
    dpre = (dact * sig * (1.0 + pre_flat * (1.0 - sig))).astype(jnp.bfloat16)
    first_list = []
    for row_shift in range(3):
        for col_shift in range(3):
            piece = input_pad[
                :, row_shift : row_shift + slab_rows, col_shift : col_shift + PCOLS
            ].reshape(-1, CIN)
            first_list.append(
                lax.dot_general(
                    piece, dpre, (((0,), (0,)), ((), ())), preferred_element_type=jnp.float32
                )
            )
    grad_first = jnp.stack(first_list, axis=1).reshape(-1, CMID)
    owned_first, owned_second = (
        lax.psum_scatter(grad_first, "wide", scatter_dimension=0, tiled=True),
        lax.psum_scatter(grad_second, "wide", scatter_dimension=0, tiled=True),
    )
    owned_first, owned_second = lax.psum((owned_first, owned_second), "head")
    squares = lax.psum(
        jnp.sum(owned_first * owned_first) + jnp.sum(owned_second * owned_second), "wide"
    )
    limit = 0.5 * math.sqrt(9 * CIN * CMID + 9 * CMID * PCH)
    factor = jnp.minimum(1.0, limit / (jnp.sqrt(squares) + norm_eps))
    kernel_one, mean_one, square_one = adam_update(
        kernel_first, mean_first, square_first, owned_first * factor
    )
    kernel_two, mean_two, square_two = adam_update(
        kernel_second, mean_second, square_second, owned_second * factor
    )
    return (input_grad_t, kernel_one, kernel_two, mean_one, mean_two, square_one, square_two)


def solution(mesh):
    in_specs = (
        P("wide", "head"),
        P("wide", "head"),
        P("wide", "head"),
        P("wide", "head"),
        P(None, "wide", "head"),
        P(),
        P(),
        P(),
        P(),
        P(None, "head"),
        P("wide", "head", None, None),
        P("wide", "head", None, None),
        P("wide", None),
        P("wide", None),
        P("wide", None),
        P("wide", None),
        P("wide", None),
        P("wide", None),
    )
    out_specs = (
        P("head", "wide"),
        P("wide", None),
        P("wide", None),
        P("wide", None),
        P("wide", None),
        P("wide", None),
        P("wide", None),
    )
    return jax.shard_map(shards, mesh=mesh, in_specs=in_specs, out_specs=out_specs, check_vma=False)
```

profile of v0, /device:TPU:0, one launch (start us, length us, event | category | flops | bytes accessed | tf_op | source)
XLA Modules:
  0.0 627.6 jit_solution(11004746859408749644)
XLA Ops:
  25.2 18.9 %collective-permute-start.1 = (bf16[2,256,1024]{1,2,0:T(8,128)(2,1)}, bf16[2,256,1024]{1,2,0:T(8,128)(2,1)}, u32[]{:S(2)}, u32[]{:S(2)}) collective-permute-start(bf16[2,256,1024]{1,2,0:T(8,128)(2,1)} %collective-permute-done), channel_id=1, source_target_pairs={{0,1},{1,2},{2,3},{3,4},{4,5},{5,6},{6,7},{7,8},{8,9},{9,10},{10,1... | collective-permute-start | bytes 3145736 | tf_op jit(solution)/shard_map/ppermute | solution.py:31
  51.2 31.9 %collective-permute-start.2 = (bf16[2,256,1024]{1,2,0:T(8,128)(2,1)}, bf16[2,256,1024]{1,2,0:T(8,128)(2,1)}, u32[]{:S(2)}, u32[]{:S(2)}) collective-permute-start(bf16[2,256,1024]{1,2,0:T(8,128)(2,1)} %collective-permute-done.1), channel_id=1, source_target_pairs={{0,1},{1,2},{2,3},{3,4},{4,5},{5,6},{6,7},{7,8},{8,9},{9,10},{10,1... | collective-permute-start | bytes 3145736 | tf_op jit(solution)/shard_map/ppermute | solution.py:31
  86.4 35.6 %collective-permute-start.3 = (bf16[2,256,1024]{1,2,0:T(8,128)(2,1)}, bf16[2,256,1024]{1,2,0:T(8,128)(2,1)}, u32[]{:S(2)}, u32[]{:S(2)}) collective-permute-start(bf16[2,256,1024]{1,2,0:T(8,128)(2,1)} %collective-permute-done.2), channel_id=1, source_target_pairs={{0,1},{1,2},{2,3},{3,4},{4,5},{5,6},{6,7},{7,8},{8,9},{9,10},{10,1... | collective-permute-start | bytes 3145736 | tf_op jit(solution)/shard_map/ppermute | solution.py:31
  133.9 10.1 %fusion.117 = (f32[8,256]{1,0:T(8,128)S(1)}, f32[8,256,1280]{1,2,0:T(8,128)}) fusion(pred[256,1280]{0,1:T(8,128)(4,1)S(1)} %and_dynamic-update-slice_fusion, bf16[1280,8,128]{2,0,1:T(8,128)(2,1)} %constant_dynamic-update-slice_fusion, bf16[256,8,128]{0,2,1:T(8,128)(2,1)} %bitcast.333), kind=kOutput, calls=%fused_computation.253 | convolution fusion | flops 684197120 | bytes 13967360 | tf_op jit(solution)/shard_map/sub | solution.py:85
  144.0 5.2 fusion.8
  155.6 6.5 %fusion.1 = bf16[8,256,1280]{1,2,0:T(8,128)(2,1)S(1)} fusion(bf16[1280,8,128]{2,0,1:T(8,128)(2,1)} %constant_dynamic-update-slice_fusion.5, bf16[256,8,128]{0,2,1:T(8,128)(2,1)S(1)} %copy-done.6, f32[8,256]{1,0:T(8,128)S(1)} %copy.165, f32[8,256,1280]{1,2,0:T(8,128)} %get-tuple-element.95, f32[8,256]{1,0:T(8,128)S(1)} %get-tuple-element.94), kind=kOutput, calls=%fused_computation.2 | convolution fusion | flops 681574400 | bytes 18890752 | tf_op jit(solution)/shard_map/qhd,khd->hqk/dot_general | solution.py:90
  167.9 4.5 convolution_bitcast_fusion.1
  186.6 26.8 %collective-permute-done.4 = f32[2,256,1024]{2,1,0:T(8,128)} collective-permute-done((f32[2,256,1024]{2,1,0:T(8,128)}, f32[2,256,1024]{2,1,0:T(8,128)}, u32[]{:S(2)}, u32[]{:S(2)}) %collective-permute-start.4) | collective-permute-done | bytes 2097184 | tf_op jit(solution)/shard_map/ppermute | solution.py:31
  223.8 22.3 %collective-permute-done.5 = f32[2,256,1024]{2,1,0:T(8,128)} collective-permute-done((f32[2,256,1024]{2,1,0:T(8,128)}, f32[2,256,1024]{2,1,0:T(8,128)}, u32[]{:S(2)}, u32[]{:S(2)}) %collective-permute-start.5) | collective-permute-done | bytes 2097184 | tf_op jit(solution)/shard_map/ppermute | solution.py:31
  246.1 4.0 maximum_add_fusion.2
  256.6 21.3 %collective-permute-done.6 = f32[2,256,1024]{2,1,0:T(8,128)} collective-permute-done((f32[2,256,1024]{2,1,0:T(8,128)}, f32[2,256,1024]{2,1,0:T(8,128)}, u32[]{:S(2)}, u32[]{:S(2)}) %collective-permute-start.6) | collective-permute-done | bytes 2097184 | tf_op jit(solution)/shard_map/ppermute | solution.py:31
  285.8 5.3 fusion.15
  293.2 16.3 %collective-permute-done.7 = f32[2,256,1024]{2,1,0:T(8,128)} collective-permute-done((f32[2,256,1024]{2,1,0:T(8,128)}, f32[2,256,1024]{2,1,0:T(8,128)}, u32[]{:S(2)}, u32[]{:S(2)}) %collective-permute-start.7) | collective-permute-done | bytes 2097184 | tf_op jit(solution)/shard_map/ppermute | solution.py:31
  312.4 13.1 %fusion.7 = bf16[4096,256]{0,1:T(8,128)(2,1)} fusion(bf16[3,4096,1024]{2,1,0:T(8,128)(2,1)} %all-gather.2.cloned.1.call-done, bf16[2,256,1024]{2,1,0:T(8,128)(2,1)} %fusion.9, bf16[1,256,1024]{2,1,0:T(8,128)(2,1)} %copy.153), kind=kOutput, calls=%fused_computation.13 | convolution fusion | flops 6444285952 | bytes 28835840 | tf_op jit(solution)/shard_map/prk,ptk->rt/dot_general | solution.py:178
  329.9 46.0 %all_gather.7 = bf16[1152,256]{1,0:T(8,128)(2,1)S(1)} all-gather(bf16[72,256]{1,0:T(8,128)(2,1)S(1)} %convert_element_type.98), channel_id=1, replica_groups=mesh['head'=2,'wide'=16] {'wide'}, dimensions={0}, use_global_device_ids=true | all-gather | bytes 626688 | tf_op jit(solution)/shard_map/all_gather | solution.py:210
  375.9 9.2 %reduce-scatter.6.cloned.1.call-done = bf16[2048,256]{0,1:T(8,128)(2,1)} async-done(((bf16[4096,256]{0,1:T(8,128)(2,1)}), bf16[2048,256]{0,1:T(8,128)(2,1)}) %reduce-scatter.6.cloned.1.call-update) | async-done | bytes 1048592 | tf_op jit(solution)/shard_map/reduce_scatter | solution.py:185
  390.4 19.1 %all-reduce.6.cloned.1.call-done = bf16[256,256]{1,0:T(8,128)(2,1)} async-done(((bf16[256,256]{1,0:T(8,128)(2,1)}), bf16[256,256]{1,0:T(8,128)(2,1)}) %all-reduce.6.cloned.1.call-update) | async-done | bytes 131088 | tf_op jit(solution)/shard_map/psum | solution.py:192
  411.0 5.6 all-to-all-start
  418.3 8.4 %all-to-all-done = bf16[16,32,256]{2,1,0:T(8,128)(2,1)S(1)} async-done(((bf16[16,32,256]{2,1,0:T(8,128)(2,1)}), bf16[16,32,256]{2,1,0:T(8,128)(2,1)S(1)}, u32[]{:S(2)}, u32[]{:S(2)}) %all-to-all-start) | async-done | bytes 262176 | tf_op jit(solution)/shard_map/all_to_all | solution.py:206
  451.3 45.6 %reduce-scatter.10.cloned.1.call-done = f32[72,128]{1,0:T(8,128)} async-done(((f32[1152,128]{1,0:T(8,128)}), f32[72,128]{1,0:T(8,128)}) %reduce-scatter.10.cloned.1.call-update) | async-done | bytes 36880
  496.9 9.0 %psum.29 = f32[72,128]{1,0:T(8,128)S(1)} all-reduce(f32[72,128]{1,0:T(8,128)} %reduce-scatter.10.cloned.1.call-done), channel_id=1, replica_groups=mesh['head'=2,'wide'=16] {'head'}, use_global_device_ids=true, to_apply=%region_25.26 | all-reduce | flops 9216 | bytes 73728 | tf_op jit(solution)/shard_map/psum | solution.py:264
  505.9 51.5 %reduce-scatter.8.cloned.1.call-done = f32[72,256]{1,0:T(8,128)} async-done(((f32[1152,256]{1,0:T(8,128)}), f32[72,256]{1,0:T(8,128)}) %reduce-scatter.8.cloned.1.call-update) | async-done | bytes 73744 | tf_op jit(solution)/shard_map/reduce_scatter | solution.py:262
  558.1 21.2 %all-reduce.8.cloned.1.call-done = f32[72,256]{1,0:T(8,128)} async-done(((f32[72,256]{1,0:T(8,128)}), f32[72,256]{1,0:T(8,128)}) %all-reduce.8.cloned.1.call-update) | async-done | bytes 73744 | tf_op jit(solution)/shard_map/psum | solution.py:264
  584.4 33.4 %psum.31 = f32[]{:T(128)} all-reduce(f32[]{:T(128)S(6)} %add.264), channel_id=1, replica_groups=mesh['head'=2,'wide'=16] {'wide'}, use_global_device_ids=true, to_apply=%region_30.31 | all-reduce | flops 1 | bytes 8 | tf_op jit(solution)/shard_map/psum | solution.py:265
  (196 shorter events, 130.7 us)
Async XLA Ops:
  7.2 378.0 %copy-start = (bf16[256,2048]{1,0:T(8,128)(2,1)S(1)}, bf16[256,2048]{1,0:T(8,128)(2,1)}, u32[]{:S(2)}) copy-start(bf16[256,2048]{1,0:T(8,128)(2,1)} %param.27) | copy-start | bytes 3145732
  7.2 305.2 %all-gather.2.cloned.1.call-start = ((), (), s32[]{:S(2)}) async-start(), calls=%async_computation.4 | async-start | bytes 26738688 | tf_op jit(solution)/shard_map/all_gather | solution.py:180
  8.0 377.2 %reduce-scatter.6.cloned.1.call-start = ((), (), s32[]{:S(2)}) async-start(), calls=%async_computation.5 | async-start | bytes 3145728 | tf_op jit(solution)/shard_map/reduce_scatter | solution.py:185
  9.6 15.6 %collective-permute-start = (bf16[2,256,1024]{1,2,0:T(8,128)(2,1)S(1)}, bf16[2,256,1024]{1,2,0:T(8,128)(2,1)}, u32[]{:S(2)}, u32[]{:S(2)}) collective-permute-start(bf16[2,256,1024]{1,2,0:T(8,128)(2,1)S(1)} %pad_maximum_fusion.1), channel_id=1, source_target_pairs={{0,1},{1,2},{2,3},{3,4},{4,5},{5,6},{6,7},{7,8},{8,9},{9,10},{10,1... | collective-permute-start | bytes 3145736 | tf_op jit(solution)/shard_map/ppermute | solution.py:31
  25.2 26.0 %collective-permute-start.1 = (bf16[2,256,1024]{1,2,0:T(8,128)(2,1)}, bf16[2,256,1024]{1,2,0:T(8,128)(2,1)}, u32[]{:S(2)}, u32[]{:S(2)}) collective-permute-start(bf16[2,256,1024]{1,2,0:T(8,128)(2,1)} %collective-permute-done), channel_id=1, source_target_pairs={{0,1},{1,2},{2,3},{3,4},{4,5},{5,6},{6,7},{7,8},{8,9},{9,10},{10,1... | collective-permute-start | bytes 3145736 | tf_op jit(solution)/shard_map/ppermute | solution.py:31
  51.2 35.3 %collective-permute-start.2 = (bf16[2,256,1024]{1,2,0:T(8,128)(2,1)}, bf16[2,256,1024]{1,2,0:T(8,128)(2,1)}, u32[]{:S(2)}, u32[]{:S(2)}) collective-permute-start(bf16[2,256,1024]{1,2,0:T(8,128)(2,1)} %collective-permute-done.1), channel_id=1, source_target_pairs={{0,1},{1,2},{2,3},{3,4},{4,5},{5,6},{6,7},{7,8},{8,9},{9,10},{10,1... | collective-permute-start | bytes 3145736 | tf_op jit(solution)/shard_map/ppermute | solution.py:31
  86.4 43.9 %collective-permute-start.3 = (bf16[2,256,1024]{1,2,0:T(8,128)(2,1)}, bf16[2,256,1024]{1,2,0:T(8,128)(2,1)}, u32[]{:S(2)}, u32[]{:S(2)}) collective-permute-start(bf16[2,256,1024]{1,2,0:T(8,128)(2,1)} %collective-permute-done.2), channel_id=1, source_target_pairs={{0,1},{1,2},{2,3},{3,4},{4,5},{5,6},{6,7},{7,8},{8,9},{9,10},{10,1... | collective-permute-start | bytes 3145736 | tf_op jit(solution)/shard_map/ppermute | solution.py:31
  180.3 33.2 %collective-permute-start.4 = (f32[2,256,1024]{2,1,0:T(8,128)}, f32[2,256,1024]{2,1,0:T(8,128)}, u32[]{:S(2)}, u32[]{:S(2)}) collective-permute-start(f32[2,256,1024]{2,1,0:T(8,128)} %pad_maximum_fusion), channel_id=1, source_target_pairs={{1,0},{2,1},{3,2},{4,3},{5,4},{6,5},{7,6},{8,7},{9,8},{10,9},{11,1... | collective-permute-start | bytes 6291464 | tf_op jit(solution)/shard_map/ppermute | solution.py:31
  217.4 28.7 %collective-permute-start.5 = (f32[2,256,1024]{2,1,0:T(8,128)}, f32[2,256,1024]{2,1,0:T(8,128)}, u32[]{:S(2)}, u32[]{:S(2)}) collective-permute-start(f32[2,256,1024]{2,1,0:T(8,128)} %maximum_add_fusion.1), channel_id=1, source_target_pairs={{1,0},{2,1},{3,2},{4,3},{5,4},{6,5},{7,6},{8,7},{9,8},{10,9},{11,1... | collective-permute-start | bytes 6291464 | tf_op jit(solution)/shard_map/ppermute | solution.py:31
  250.2 27.7 %collective-permute-start.6 = (f32[2,256,1024]{2,1,0:T(8,128)}, f32[2,256,1024]{2,1,0:T(8,128)}, u32[]{:S(2)}, u32[]{:S(2)}) collective-permute-start(f32[2,256,1024]{2,1,0:T(8,128)} %maximum_add_fusion.2), channel_id=1, source_target_pairs={{1,0},{2,1},{3,2},{4,3},{5,4},{6,5},{7,6},{8,7},{9,8},{10,9},{11,1... | collective-permute-start | bytes 6291464 | tf_op jit(solution)/shard_map/ppermute | solution.py:31
  281.9 27.7 %collective-permute-start.7 = (f32[2,256,1024]{2,1,0:T(8,128)}, f32[2,256,1024]{2,1,0:T(8,128)}, u32[]{:S(2)}, u32[]{:S(2)}) collective-permute-start(f32[2,256,1024]{2,1,0:T(8,128)} %maximum_add_fusion.3), channel_id=1, source_target_pairs={{1,0},{2,1},{3,2},{4,3},{5,4},{6,5},{7,6},{8,7},{9,8},{10,9},{11,1... | collective-permute-start | bytes 6291464 | tf_op jit(solution)/shard_map/ppermute | solution.py:31
  325.5 84.0 %all-reduce.6.cloned.1.call-start = ((), (), s32[]{:S(2)}) async-start(), calls=%async_computation.6 | async-start | bytes 262144 | tf_op jit(solution)/shard_map/psum | solution.py:192
  325.6 92.6 %collective-permute-start.8 = (bf16[2,1,1,8,128]{4,3,2,1,0:T(8,128)(2,1)S(1)}, bf16[2,1,1,8,128]{4,3,2,1,0:T(8,128)(2,1)S(1)}, u32[]{:S(2)}, u32[]{:S(2)}) collective-permute-start(bf16[2,1,1,8,128]{4,3,2,1,0:T(8,128)(2,1)S(1)} %get-tuple-element.90), channel_id=1, source_target_pairs={{0,16},{1,17},{2,18},{3,19},{4,20},{5,21},{6,22},{7,23},{8,24},{9,... | collective-permute-start | bytes 12296 | tf_op jit(solution)/shard_map/ppermute | solution.py:42
  328.6 89.7 %collective-permute-start.9 = (bf16[2,1,1,8,128]{4,3,2,1,0:T(8,128)(2,1)S(1)}, bf16[2,1,1,8,128]{4,3,2,1,0:T(8,128)(2,1)S(1)}, u32[]{:S(2)}, u32[]{:S(2)}) collective-permute-start(bf16[2,1,1,8,128]{4,3,2,1,0:T(8,128)(2,1)S(1)} %get-tuple-element.91), channel_id=1, source_target_pairs={{16,0},{17,1},{18,2},{19,3},{20,4},{21,5},{22,6},{23,7},{24,8},{25... | collective-permute-start | bytes 12296 | tf_op jit(solution)/shard_map/ppermute | solution.py:44
  411.0 15.7 %all-to-all-start = ((bf16[16,32,256]{2,1,0:T(8,128)(2,1)}), bf16[16,32,256]{2,1,0:T(8,128)(2,1)S(1)}, u32[]{:S(2)}, u32[]{:S(2)}) async-start(bf16[16,32,256]{2,1,0:T(8,128)(2,1)} %broadcast_select_fusion), calls=%async_computation.1 | async-start | bytes 524288 | tf_op jit(solution)/shard_map/all_to_all | solution.py:206
  416.7 80.3 %reduce-scatter.10.cloned.1.call-start = ((), (), s32[]{:S(2)}) async-start(), calls=%async_computation.9 | async-start | bytes 626688
  430.4 4.6 collective-permute-start.10
  432.8 5.5 collective-permute-start.11
  444.5 112.9 %reduce-scatter.8.cloned.1.call-start = ((), (), s32[]{:S(2)}) async-start(), calls=%async_computation.7 | async-start | bytes 1253376 | tf_op jit(solution)/shard_map/reduce_scatter | solution.py:262
  450.0 168.4 %copy-start.13 = (f32[72,128]{1,0:T(8,128)S(1)}, f32[72,128]{1,0:T(8,128)}, u32[]{:S(2)}) copy-start(f32[72,128]{1,0:T(8,128)} %param.30) | copy-start | bytes 110596
  450.0 168.4 %copy-start.14 = (f32[72,128]{1,0:T(8,128)S(1)}, f32[72,128]{1,0:T(8,128)}, u32[]{:S(2)}) copy-start(f32[72,128]{1,0:T(8,128)} %param.32) | copy-start | bytes 110596
  450.0 168.4 %copy-start.15 = (f32[72,128]{1,0:T(8,128)S(1)}, f32[72,128]{1,0:T(8,128)}, u32[]{:S(2)}) copy-start(f32[72,128]{1,0:T(8,128)} %param.34) | copy-start | bytes 110596
  451.3 167.9 %copy-start.12 = (f32[72,256]{1,0:T(8,128)S(1)}, f32[72,256]{1,0:T(8,128)}, u32[]{:S(2)}) copy-start(f32[72,256]{1,0:T(8,128)} %param.35) | copy-start | bytes 221188
  451.3 128.0 %all-reduce.8.cloned.1.call-start = ((), (), s32[]{:S(2)}) async-start(), calls=%async_computation.8 | async-start | bytes 147456 | tf_op jit(solution)/shard_map/psum | solution.py:264
  (17 other events, 416.8 us)
Sparse Core Ops, SparseCore 0:
  9.6 168.3 all-gather.1
  325.7 59.4 reduce-scatter.5
  388.0 21.4 all-reduce.5
  444.7 52.2 reduce-scatter.9
  500.4 56.9 reduce-scatter.7
  559.5 19.6 all-reduce.7
where the time goes:
time: 629 us; the launch traced here: 628 us
  waiting for transfers between devices  246 us (39%)
  starting transfers between devices  109 us (17%)
  blocking collectives  88.3 us (14%)
  local copies, waits for them, and re-layouts  62.7 us (10%)
  matrix products  57.5 us (9%)
  other arithmetic  38.3 us (6%)
  between operations  26 us (4%)
    ppermute x8, starting transfers between devices, passed_along(): return lax.ppermute(block, axis, route)  95 us
    ppermute x8, waiting for transfers between devices, passed_along(): return lax.ppermute(block, axis, route)  86.7 us
    reduce_scatter x1, waiting for transfers between devices, shards(): lax.psum_scatter(grad_second, 'wide', scatter_dimension=0, tiled=True)  51.5 us
    unnamed x7, waiting for transfers between devices  46.4 us
    all_gather x1, blocking collectives, shards(): lax.all_gather(kernel_second.astype(jnp.bfloat16), 'wide', axis=0, tiled=...  46 us
    psum x1, blocking collectives, shards(): lax.psum(jnp.sum(owned_first * owned_first) + jnp.sum(owned_second * owne...  33.4 us
    another operation x10, local copies, waits for them, and re-layouts, shards(): jnp.stack([dkey[offset * tokens_here:(offset + 1) * tokens_here], dvalue[...  21.9 us
    psum x1, waiting for transfers between devices, shards(): owned_first, owned_second = lax.psum((owned_first, owned_second), 'head')  21.2 us
  transfers between devices with their start and end apart: 19, of which 11 were waited for; matrix products, arithmetic and copies ran while one was open for 20% of the time, Pallas kernels for 0%

commit v1 on v0

v1 whole, which is shorter than its diff:
```python
import functools
import math

import jax
import jax.numpy as jnp
from jax import lax
from jax.experimental import pallas as pl
from jax.experimental.pallas import tpu as pltpu
from jax.sharding import PartitionSpec as P

HD = 128
REACH = 4
PROWS = 8
PCOLS = 8
PCH = 256
CMID = 128
CIN = 128
IMGTOK = 64


neg_big = -1e30
beta_one = 0.9
beta_two = 0.95
adam_eps = 1e-08
learn_rate = 0.02
decay_rate = 0.1
adam_step = 10
norm_eps = 1e-06


def passed_along(block, axis, distance):
    devices = range(lax.axis_size(axis))
    route = [(i - distance, i) for i in devices if i - distance in devices]
    return lax.ppermute(block, axis, route)


def with_halo(cells, sides, width):
    for axis, dim in sides:
        count = lax.axis_size(axis)
        ends = count - 1
        head = lax.slice_in_dim(cells, 0, width, axis=dim)
        tail = lax.slice_in_dim(cells, cells.shape[dim] - width, cells.shape[dim], axis=dim)
        cells = jnp.concatenate(
            [
                lax.ppermute(tail, axis, [(i, (i + 1) % count) for i in range(ends)]),
                cells,
                lax.ppermute(head, axis, [((i + 1) % count, i) for i in range(ends)]),
            ],
            axis=dim,
        )
    return cells


def pick_entry(lookup, wanted):
    return jnp.sum(jnp.where(jnp.arange(lookup.shape[0]) == wanted, lookup, 0))


def doc_number(places, doc_lengths):
    ends = jnp.cumsum(doc_lengths)
    return jnp.sum((places[:, None] >= ends[None, :]).astype(jnp.int32), axis=1)


def image_number(block, local, image_count, image_offset):
    present = pick_entry(image_count, block)
    start = pick_entry(image_offset, block)
    inside = (present > 0) & (local >= start) & (local < start + IMGTOK)
    return jnp.where(inside, block, -1)


def allowed_mask(query_places, query_docs, query_images, key_places, key_docs, key_images):
    same_doc = query_docs[:, None] == key_docs[None, :]
    earlier = key_places[None, :] <= query_places[:, None]
    same_image = (query_images[:, None] == key_images[None, :]) & (query_images[:, None] >= 0)
    return same_doc & (earlier | same_image)


def attend_block(query, key_all, value_all, grad_out, allowed):
    scale = 1.0 / math.sqrt(HD)
    rows = query.shape[0]
    count = key_all.shape[0]
    query_h = query.reshape(rows, -1, HD)
    key_h = key_all.reshape(count, -1, HD)
    value_h = value_all.reshape(count, -1, HD)
    grad_h = grad_out.reshape(rows, -1, HD)
    scores = jnp.einsum("qhd,khd->hqk", query_h, key_h, preferred_element_type=jnp.float32) * scale
    scores = jnp.where(allowed[None], scores, neg_big)
    top = jnp.max(scores, axis=-1, keepdims=True)
    expo = jnp.where(allowed[None], jnp.exp(scores - top), 0.0)
    prob = expo / jnp.sum(expo, axis=-1, keepdims=True)
    prob_low = prob.astype(jnp.bfloat16)
    output = jnp.einsum("hqk,khd->qhd", prob_low, value_h, preferred_element_type=jnp.float32)
    delta = jnp.einsum("qhd,qhd->hq", grad_h.astype(jnp.float32), output)
    dprob = jnp.einsum("qhd,khd->hqk", grad_h, value_h, preferred_element_type=jnp.float32)
    dscore = (prob * (dprob - delta[:, :, None])).astype(jnp.bfloat16)
    dquery = jnp.einsum("hqk,khd->qhd", dscore, key_h, preferred_element_type=jnp.float32) * scale
    dkey = jnp.einsum("hqk,qhd->khd", dscore, query_h, preferred_element_type=jnp.float32) * scale
    dvalue = jnp.einsum("hqk,qhd->khd", prob_low, grad_h, preferred_element_type=jnp.float32)
    return (dquery.reshape(rows, -1), dkey.reshape(count, -1), dvalue.reshape(count, -1))


def adam_update(param, mean, square, grad):
    new_mean = beta_one * mean + (1.0 - beta_one) * grad
    new_square = beta_two * square + (1.0 - beta_two) * grad * grad
    fixed_mean = new_mean / (1.0 - beta_one**adam_step)
    fixed_square = new_square / (1.0 - beta_two**adam_step)
    new_param = param - learn_rate * (
        fixed_mean / (jnp.sqrt(fixed_square) + adam_eps) + decay_rate * param
    )
    return (new_param, new_mean, new_square)


def window_start(place, reach):
    return max(place, 1) - reach if place <= reach - 2 else 1


def attend_kernel(reach, x_ref, prev_ref, key_doc, key_img, query_doc, query_img, dq_ref, dkv_ref,
                  back_ref, keys, vals, dkeys, dvals):
    scale = 1.0 / math.sqrt(HD)
    rows = x_ref.shape[2]
    front = reach - 1
    for block in range(front):
        keys[block * rows : (block + 1) * rows] = prev_ref[block, 0]
        vals[block * rows : (block + 1) * rows] = prev_ref[block, 1]
    for block in range(reach):
        at = (front + block) * rows
        keys[at : at + rows] = x_ref[block, 1]
        vals[at : at + rows] = x_ref[block, 2]
    dkeys[...] = jnp.zeros_like(dkeys)
    dvals[...] = jnp.zeros_like(dvals)
    for place in range(reach):
        low = (front + window_start(place, reach)) * rows
        high = (front + place + 1) * rows
        query = x_ref[place, 0]
        grad_out = x_ref[place, 3]
        here = slice(place * rows, (place + 1) * rows)
        qdoc = query_doc[:, here]
        qimg = query_img[:, here]
        key_at = lax.broadcasted_iota(jnp.int32, (high - low, rows), 0) + low
        query_at = lax.broadcasted_iota(jnp.int32, (high - low, rows), 1) + (front + place) * rows
        allowed = (key_doc[low:high] == qdoc) & (
            (key_at <= query_at) | ((key_img[low:high] == qimg) & (qimg >= 0))
        )
        key = keys[low:high]
        across = (((1,), (1,)), ((), ()))
        scores = lax.dot_general(key, query, across, preferred_element_type=jnp.float32) * scale
        scores = jnp.where(allowed, scores, neg_big)
        expo = jnp.exp(scores - jnp.max(scores, axis=0, keepdims=True))
        prob = expo * (1.0 / jnp.sum(expo, axis=0, keepdims=True))
        prob_low = prob.astype(jnp.bfloat16)
        dprob = lax.dot_general(vals[low:high], grad_out, across, preferred_element_type=jnp.float32)
        delta = jnp.sum(prob_low.astype(jnp.float32) * dprob, axis=0, keepdims=True)
        dscore = (prob * (dprob - delta)).astype(jnp.bfloat16)
        dq = lax.dot_general(
            dscore, key, (((0,), (0,)), ((), ())), preferred_element_type=jnp.float32
        )
        dq_ref[place] = (dq * scale).astype(jnp.bfloat16)
        dkeys[low:high] += jnp.dot(dscore, query, preferred_element_type=jnp.float32) * scale
        dvals[low:high] += jnp.dot(prob_low, grad_out, preferred_element_type=jnp.float32)
    for block in range(front):
        here = slice(block * rows, (block + 1) * rows)
        back_ref[block, 0] = dkeys[here].astype(jnp.bfloat16)
        back_ref[block, 1] = dvals[here].astype(jnp.bfloat16)
    for block in range(reach):
        here = slice((front + block) * rows, (front + block + 1) * rows)
        dkv_ref[block, 0] = dkeys[here]
        dkv_ref[block, 1] = dvals[here]


def attend_heads(queries, keys, values, out_grad, doc_lengths, image_count, image_offset):
    rows, width = queries.shape
    wide_count = lax.axis_size("wide")
    device_index = lax.axis_index("wide")
    reach = REACH
    front = reach - 1
    part = width // reach
    groups = [[g * reach + i for i in range(reach)] for g in range(wide_count // reach)]
    packed = jnp.stack([queries, keys, values, out_grad]).reshape(4, rows, reach, part)
    packed = packed.transpose(2, 0, 1, 3)
    mine = lax.all_to_all(
        packed, "wide", split_axis=0, concat_axis=0, tiled=True, axis_index_groups=groups
    )
    prev = passed_along(mine[1:, 1:3], "wide", reach)
    first_block = device_index // reach * reach - front
    place = first_block * rows + jnp.arange((front + reach) * rows, dtype=jnp.int32)
    block = place // rows
    present = jnp.zeros_like(place)
    start = jnp.zeros_like(place)
    for b in range(wide_count):
        present = jnp.where(block == b, image_count[b], present)
        start = jnp.where(block == b, image_offset[b], start)
    local = place - block * rows
    inside = (place >= 0) & (present > 0) & (local >= start) & (local < start + IMGTOK)
    image = jnp.where(inside, block, -1)
    doc = jnp.where(place >= 0, doc_number(place, doc_lengths), -1)
    total = (front + reach) * rows
    heads = part // HD

    def by_head(*lead):
        return pl.BlockSpec((*lead, rows, HD), lambda h: (0,) * (len(lead) + 1) + (h,))

    def same(shape):
        return pl.BlockSpec(shape, lambda h: (0, 0))

    dq, dkv, back = pl.pallas_call(
        functools.partial(attend_kernel, reach),
        grid=(heads,),
        in_specs=[
            by_head(reach, 4),
            by_head(front, 2),
            same((total, 1)),
            same((total, 1)),
            same((1, reach * rows)),
            same((1, reach * rows)),
        ],
        out_specs=[by_head(reach), by_head(reach, 2), by_head(front, 2)],
        out_shape=[
            jax.ShapeDtypeStruct((reach, rows, part), jnp.bfloat16),
            jax.ShapeDtypeStruct((reach, 2, rows, part), jnp.float32),
            jax.ShapeDtypeStruct((front, 2, rows, part), jnp.bfloat16),
        ],
        scratch_shapes=[
            pltpu.VMEM((total, HD), jnp.bfloat16),
            pltpu.VMEM((total, HD), jnp.bfloat16),
            pltpu.VMEM((total, HD), jnp.float32),
            pltpu.VMEM((total, HD), jnp.float32),
        ],
        compiler_params=pltpu.CompilerParams(vmem_limit_bytes=40 * 1024 * 1024),
        cost_estimate=pl.CostEstimate(
            flops=heads * 17 * rows * rows * HD * 10,
            bytes_accessed=total * part * 24,
            transcendentals=heads * 17 * rows * rows,
        ),
    )(
        mine,
        prev,
        doc[:, None],
        image[:, None],
        doc[None, front * rows :],
        image[None, front * rows :],
    )
    late = passed_along(back, "wide", -reach).astype(jnp.float32)
    dkv = jnp.concatenate([dkv[:1], dkv[1:] + late], axis=0).astype(jnp.bfloat16)
    grads = jnp.concatenate([dq[:, None], dkv], axis=1)
    grads = lax.all_to_all(
        grads, "wide", split_axis=0, concat_axis=0, tiled=True, axis_index_groups=groups
    )
    return grads.transpose(1, 2, 0, 3).reshape(3, rows, width)


def attend_ring(queries, keys, values, out_grad, doc_lengths, image_count, image_offset):
    tokens_here = queries.shape[0]
    wide_count = lax.axis_size("wide")
    device_index = lax.axis_index("wide")
    local_places = jnp.arange(tokens_here, dtype=jnp.int32)
    query_places = device_index * tokens_here + local_places
    query_docs = doc_number(query_places, doc_lengths)
    query_images = image_number(device_index, local_places, image_count, image_offset)
    own_block = jnp.stack([keys, values])
    blocks = [own_block]
    moving = own_block
    for offset in range(REACH):
        moving = passed_along(moving, "wide", 1)
        blocks.append(moving)
    masks = []
    for offset in range(REACH + 1):
        source = (device_index - offset) % wide_count
        key_places = source * tokens_here + local_places
        key_docs = doc_number(key_places, doc_lengths)
        key_images = image_number(source, local_places, image_count, image_offset)
        visible = allowed_mask(
            query_places, query_docs, query_images, key_places, key_docs, key_images
        )
        masks.append(visible & (device_index - offset >= 0))
    allowed = jnp.concatenate(masks, axis=1)
    key_all = jnp.concatenate([block[0] for block in blocks], axis=0)
    value_all = jnp.concatenate([block[1] for block in blocks], axis=0)
    dquery, dkey, dvalue = attend_block(queries, key_all, value_all, out_grad, allowed)
    parts = [
        jnp.stack(
            [
                dkey[offset * tokens_here : (offset + 1) * tokens_here],
                dvalue[offset * tokens_here : (offset + 1) * tokens_here],
            ]
        )
        for offset in range(REACH + 1)
    ]
    carried = jnp.zeros_like(parts[0])
    for offset in range(REACH):
        carried = passed_along(carried + parts[REACH - offset], "wide", -1)
    key_grads = parts[0] + carried
    return jnp.stack(
        [
            dquery.astype(jnp.bfloat16),
            key_grads[0].astype(jnp.bfloat16),
            key_grads[1].astype(jnp.bfloat16),
        ]
    )
def tail_kernel(slab_ref, seg_ref, klow_ref, act_t, in_t, pre_ref, kern1, kern2, mean1, mean2, sq1, sq2,
                o_k1, o_k2, o_m1, o_m2, o_s1, o_s2,
                seg_all, klow_all, out_seg, seg_in, grads, grads_in, total_all, norm_all,
                sem_hs, sem_hr, sem_ks, sem_kr, sem_ss, sem_sr, sem_gs, sem_gr, sem_ts, sem_tr, sem_ns, sem_nr):
    heads, wide = seg_all.shape[0], klow_all.shape[0]
    me, head = lax.axis_index("wide"), lax.axis_index("head")
    slab = pre_ref.shape[0]
    send_rows = out_seg.shape[0]
    pad = klow_all.shape[1]
    chunk = kern1.shape[0]

    def go(axis, mine, count, source, dest, send, recv):
        def one(d, c):
            peer = lax.rem(mine + d, count)
            pltpu.make_async_remote_copy(
                src_ref=source(peer), dst_ref=dest.at[mine], send_sem=send.at[peer],
                recv_sem=recv.at[mine], device_id={axis: peer},
                device_id_type=pl.DeviceIdType.MESH,
            ).start()
            return c

        lax.fori_loop(1, count, one, 0)

    def done(axis, mine, count, source, dest, send, recv):
        def one(d, c):
            peer = lax.rem(mine + d, count)
            copy = pltpu.make_async_remote_copy(
                src_ref=source(peer), dst_ref=dest.at[peer], send_sem=send.at[peer],
                recv_sem=recv.at[peer], device_id={axis: peer},
                device_id_type=pl.DeviceIdType.MESH,
            )
            copy.wait_send()
            copy.wait_recv()
            return c

        lax.fori_loop(1, count, one, 0)

    barrier = pltpu.get_barrier_semaphore()

    def hello(axis, mine, count):
        def one(d, c):
            pl.semaphore_signal(barrier, inc=1, device_id={axis: lax.rem(mine + d, count)},
                                device_id_type=pl.DeviceIdType.MESH)
            return c

        lax.fori_loop(1, count, one, 0)

    hello("head", head, heads)
    hello("wide", me, wide)
    pl.semaphore_wait(barrier, heads + wide - 2)

    seg_all[head] = seg_ref[...]
    by_head = ("head", head, heads, lambda p: seg_all.at[head], seg_all, sem_hs, sem_hr)
    go(*by_head)
    klow_all[me] = klow_ref[...]
    by_kern = ("wide", me, wide, lambda p: klow_all.at[me], klow_all, sem_ks, sem_kr)
    go(*by_kern)
    done(*by_head)
    rows = pl.ds(pl.multiple_of(head * slab, 8), send_rows)
    seg = seg_all[0, rows]
    for h in range(1, heads):
        seg = seg + seg_all[h, rows]
    out_seg[...] = seg.astype(jnp.bfloat16)
    by_seg = ("wide", me, wide, lambda p: out_seg, seg_in, sem_ss, sem_sr)
    go(*by_seg)
    seg_in[me] = out_seg[...]
    done(*by_kern)
    cmid = pre_ref.shape[1]
    flat = klow_all[...].reshape(wide * pad, klow_all.shape[2])
    middle = chunk // 9
    row = lax.broadcasted_iota(jnp.int32, (cmid, wide * pad), 0)
    col = lax.broadcasted_iota(jnp.int32, (cmid, wide * pad), 1)
    place = row // middle * pad + row % middle * 9
    second = []
    for o in range(9):
        pick = (col == place + o).astype(jnp.float32).astype(jnp.bfloat16)
        second.append(
            jnp.dot(pick, flat, preferred_element_type=jnp.float32).astype(jnp.bfloat16)
        )
    done(*by_seg)
    incoming = jnp.zeros((send_rows, seg_in.shape[2]), jnp.float32)
    for n in range(wide):
        chosen = jnp.where(slab_ref[n] == me, 1.0, 0.0)
        incoming = incoming + seg_in[n].astype(jnp.float32) * chosen
    column = lax.broadcasted_iota(jnp.int32, incoming.shape, 0) % PCOLS
    shifted = [
        jnp.where(column < PCOLS - 1, pltpu.roll(incoming, send_rows - 1, 0), 0.0),
        incoming,
        jnp.where(column > 0, pltpu.roll(incoming, 1, 0), 0.0),
    ]
    dact = jnp.zeros((slab, cmid), jnp.float32)
    for o in range(9):
        start = PCOLS * (2 - o // 3)
        moved = shifted[o % 3][start : start + slab].astype(jnp.bfloat16)
        dact = dact + lax.dot_general(
            moved, second[o], (((1,), (1,)), ((), ())), preferred_element_type=jnp.float32
        )
    pre = pre_ref[...].astype(jnp.float32)
    sig = 1.0 / (1.0 + jnp.exp(-pre))
    dpre = (dact * sig * (1.0 + pre * (1.0 - sig))).astype(jnp.bfloat16)
    middle_in = incoming[PCOLS : PCOLS + slab].astype(jnp.bfloat16)
    width1 = dpre.shape[1]
    width2 = middle_in.shape[1]
    for w in range(wide):
        grads[w, :, :width1] = jnp.dot(
            in_t[w], dpre, preferred_element_type=jnp.float32
        ).astype(jnp.bfloat16)
        grads[w, :, width1:] = jnp.dot(
            act_t[w], middle_in, preferred_element_type=jnp.float32
        ).astype(jnp.bfloat16)
    by_grad = ("wide", me, wide, lambda p: grads.at[p], grads_in, sem_gs, sem_gr)
    go(*by_grad)
    grads_in[me] = grads[me]
    done(*by_grad)
    total = grads_in[0].astype(jnp.float32)
    for w in range(1, wide):
        total = total + grads_in[w].astype(jnp.float32)
    total_all[head] = total
    by_total = ("head", head, heads, lambda p: total_all.at[head], total_all, sem_ts, sem_tr)
    go(*by_total)
    done(*by_total)
    total = total_all[0]
    for h in range(1, heads):
        total = total + total_all[h]
    square = jnp.sum(total * total, axis=0, keepdims=True)
    square = jnp.sum(square, axis=1, keepdims=True)
    norm_all[me] = jnp.broadcast_to(square, norm_all.shape[1:])
    by_norm = ("wide", me, wide, lambda p: norm_all.at[me], norm_all, sem_ns, sem_nr)
    go(*by_norm)
    done(*by_norm)
    squares = norm_all[0]
    for w in range(1, wide):
        squares = squares + norm_all[w]
    squares = squares[:1, :1]
    limit = 0.5 * math.sqrt(wide * chunk * (width1 + width2))
    factor = jnp.minimum(1.0, limit / (jnp.sqrt(squares) + norm_eps))
    total = total * factor
    o_k1[...], o_m1[...], o_s1[...] = adam_update(
        kern1[...], mean1[...], sq1[...], total[:chunk, :width1]
    )
    o_k2[...], o_m2[...], o_s2[...] = adam_update(
        kern2[...], mean2[...], sq2[...], total[:chunk, width1:]
    )


def conv_update(seg, slab_owner, act, conv_input, pre_act, params):
    wide = lax.axis_size("wide")
    heads = lax.axis_size("head")
    slab_rows = pre_act.shape[1]
    slab = slab_rows * PCOLS
    kern1, kern2 = params[0], params[1]
    chunk = kern1.shape[0]
    pad = (chunk + 15) // 16 * 16
    send_rows = (slab + 2 * PCOLS + 15) // 16 * 16
    seg_rows = (heads - 1) * slab + send_rows
    seg = jnp.pad(seg, ((PCOLS, seg_rows - PCOLS - seg.shape[0]), (0, 0)))
    klow = jnp.pad(kern2.astype(jnp.bfloat16), ((0, pad - chunk), (0, 0)))
    both = with_halo(jnp.stack([conv_input, act]), (("head", 2),), 1)
    rims = jnp.pad(both, ((0, 0), (0, 0), (0, 0), (1, 1), (0, 0)))
    pieces = jnp.stack(
        [
            rims[:, 0, r : r + slab_rows, c : c + PCOLS].reshape(2, slab, -1)
            for r in range(3)
            for c in range(3)
        ],
        axis=1,
    )
    pieces = pieces.transpose(0, 3, 1, 2).reshape(2, wide, chunk, slab)
    pieces = jnp.pad(pieces, ((0, 0), (0, 0), (0, pad - chunk), (0, 0)))
    pch = kern2.shape[1]
    both_width = pch + kern1.shape[1]
    vmem = pl.BlockSpec(memory_space=pltpu.VMEM)
    dma = pltpu.SemaphoreType.DMA
    low, full = jnp.bfloat16, jnp.float32
    return pl.pallas_call(
        tail_kernel,
        in_specs=[pl.BlockSpec(memory_space=pltpu.SMEM)] + [vmem] * 11,
        out_specs=[vmem] * 6,
        out_shape=[jax.ShapeDtypeStruct(p.shape, p.dtype) for p in params],
        scratch_shapes=[
            pltpu.VMEM((heads, seg_rows, pch), full),
            pltpu.VMEM((wide, pad, pch), low),
            pltpu.VMEM((send_rows, pch), low),
            pltpu.VMEM((wide, send_rows, pch), low),
            pltpu.VMEM((wide, pad, both_width), low),
            pltpu.VMEM((wide, pad, both_width), low),
            pltpu.VMEM((heads, pad, both_width), full),
            pltpu.VMEM((wide, 8, 128), full),
        ]
        + [dma((n,)) for n in (heads, wide, wide, wide, heads, wide) for _ in range(2)],
        compiler_params=pltpu.CompilerParams(
            collective_id=0, has_side_effects=True, vmem_limit_bytes=32 * 1024 * 1024
        ),
        cost_estimate=pl.CostEstimate(
            flops=10**9, bytes_accessed=4 * 10**6, transcendentals=10**4
        ),
    )(slab_owner, seg, klow, pieces[1], pieces[0], pre_act.reshape(slab, -1), *params)


def shards(
    queries,
    keys,
    values,
    out_grad,
    qkv_weight,
    doc_lengths,
    image_count,
    image_offset,
    slab_owner,
    patch_weight,
    conv_input,
    pre_act,
    kernel_first,
    kernel_second,
    mean_first,
    mean_second,
    square_first,
    square_second,
):
    device_index = lax.axis_index("wide")
    heads_here = queries.shape[1] // HD
    wide_count = lax.axis_size("wide")
    split = heads_here % REACH == 0 and wide_count % REACH == 0
    grads = (attend_heads if split else attend_ring)(
        queries, keys, values, out_grad, doc_lengths, image_count, image_offset
    )
    partial_value = jnp.einsum(
        "prk,ptk->rt",
        lax.all_gather(qkv_weight, "wide", axis=1, tiled=True),
        grads,
        preferred_element_type=jnp.float32,
    ).astype(jnp.bfloat16)
    input_grad_t = (
        lax.psum_scatter(partial_value, "head", scatter_dimension=0, tiled=True)
        .astype(jnp.float32)
        .astype(jnp.bfloat16)
    )
    patch_part = lax.dot_general(
        input_grad_t, patch_weight, (((0,), (1,)), ((), ())), preferred_element_type=jnp.float32
    )
    has_image = pick_entry(image_count, device_index)
    offset_here = pick_entry(image_offset, device_index)
    segment = lax.dynamic_slice_in_dim(patch_part, offset_here, IMGTOK, 0)
    segment = segment * has_image.astype(jnp.float32)
    act = jax.nn.silu(pre_act.astype(jnp.float32)).astype(jnp.bfloat16)
    updated = conv_update(
        segment,
        slab_owner,
        act,
        conv_input,
        pre_act,
        (kernel_first, kernel_second, mean_first, mean_second, square_first, square_second),
    )
    kernel_one, kernel_two, mean_one, mean_two, square_one, square_two = updated
    return (input_grad_t, kernel_one, kernel_two, mean_one, mean_two, square_one, square_two)


def solution(mesh):
    in_specs = (
        P("wide", "head"),
        P("wide", "head"),
        P("wide", "head"),
        P("wide", "head"),
        P(None, "wide", "head"),
        P(),
        P(),
        P(),
        P(),
        P(None, "head"),
        P("wide", "head", None, None),
        P("wide", "head", None, None),
        P("wide", None),
        P("wide", None),
        P("wide", None),
        P("wide", None),
        P("wide", None),
        P("wide", None),
    )
    out_specs = (
        P("head", "wide"),
        P("wide", None),
        P("wide", None),
        P("wide", None),
        P("wide", None),
        P("wide", None),
        P("wide", None),
    )
    return jax.shard_map(shards, mesh=mesh, in_specs=in_specs, out_specs=out_specs, check_vma=False)
```

time: 629 us -> 305 us (0.48)
  waiting for transfers between devices: 246 us -> 98.9 us
  starting transfers between devices: 109 us -> 12 us
  Pallas kernels: 0 us -> 75.6 us
  blocking collectives: 88.3 us -> 22.5 us
  local copies, waits for them, and re-layouts: 62.7 us -> 15.4 us
  matrix products: 57.5 us -> 14.7 us
  other arithmetic: 38.3 us -> 47.8 us
  between operations: 26 us -> 17.1 us
    ppermute x8 -> x2, starting transfers between devices: 95 us -> 2.94 us  [passed_along(): return lax.ppermute(block, axis, route)]
    pallas_call x0 -> x2, Pallas kernels: none -> 75.6 us  [the longest x1 62.8 us: conv_update(): pl.pallas_call(tail_kernel, in_specs=[pl.BlockSpec(memory_space=pltpu.SME...]
    reduce_scatter x1 -> x0, waiting for transfers between devices: 51.5 us -> none  [shards(): lax.psum_scatter(grad_second, 'wide', scatter_dimension=0, tiled=True)]
    all_gather x1 -> x0, blocking collectives: 46 us -> none  [shards(): lax.all_gather(kernel_second.astype(jnp.bfloat16), 'wide', axis=0, tiled=...]
    unnamed x7 -> x2, waiting for transfers between devices: 46.4 us -> 0.7 us
    psum x2 -> x0, blocking collectives: 42.4 us -> none  [the longest x1 33.4 us: shards(): lax.psum(jnp.sum(owned_first * owned_first) + jnp.sum(owned_second * owne...]
    psum x2 -> x0, waiting for transfers between devices: 40.3 us -> none  [the longest x1 21.2 us: shards(): owned_first, owned_second = lax.psum((owned_first, owned_second), 'head')]
    ppermute x8 -> x2, waiting for transfers between devices: 86.7 us -> 46.6 us  [passed_along(): return lax.ppermute(block, axis, route)]
  transfers between devices with their start and end apart: 19 -> 7, of which waited for: 11 -> 5; matrix products, arithmetic and copies ran while one was open for 20% -> 19% of each run, Pallas kernels for 0% -> 4%
where the time goes in v1:
time: 305 us; the launch traced here: 304 us
  waiting for transfers between devices  98.9 us (32%)
  Pallas kernels  75.6 us (25%)
  other arithmetic  47.8 us (16%)
  blocking collectives  22.5 us (7%)
  between operations  17.1 us (6%)
  local copies, waits for them, and re-layouts  15.4 us (5%)
  matrix products  14.7 us (5%)
  starting transfers between devices  12 us (4%)
    pallas_call x1, Pallas kernels, conv_update(): pl.pallas_call(tail_kernel, in_specs=[pl.BlockSpec(memory_space=pltpu.SME...  62.8 us
    ppermute x2, waiting for transfers between devices, passed_along(): return lax.ppermute(block, axis, route)  46.6 us
    all_to_all x1, waiting for transfers between devices, attend_heads(): lax.all_to_all(packed, 'wide', split_axis=0, concat_axis=0, tiled=True, a...  27.5 us
    select_n x2, other arithmetic, attend_heads(): image = jnp.where(inside, block, -1)  24.2 us
    reduce_scatter x1, waiting for transfers between devices, shards(): lax.psum_scatter(partial_value, 'head', scatter_dimension=0, tiled=True)  23.2 us
    all_to_all x1, blocking collectives, attend_heads(): lax.all_to_all(grads, 'wide', split_axis=0, concat_axis=0, tiled=True, ax...  22.5 us
    dot_general x1, matrix products, shards(): jnp.einsum('prk,ptk->rt', lax.all_gather(qkv_weight, 'wide', axis=1, tile...  13 us
    pallas_call x1, Pallas kernels, attend_heads(): pl.pallas_call(functools.partial(attend_kernel, reach), grid=(heads,), in...  12.8 us
  transfers between devices with their start and end apart: 7, of which 5 were waited for; matrix products, arithmetic and copies ran while one was open for 19% of the time, Pallas kernels for 4%

profile of v1, /device:TPU:0, one launch (start us, length us, event | category | flops | bytes accessed | tf_op | source)
XLA Modules:
  0.0 304.0 jit_solution(8225794242153469094)
XLA Ops:
  7.9 1.2 copy.73
  9.8 1.2 copy.75
  11.3 1.2 copy.76
  13.5 2.7 maximum_bitcast_fusion
  16.2 4.4 %all-to-all-start = ((bf16[4,4,256,256]{3,2,1,0:T(8,128)(2,1)}), bf16[4,4,256,256]{3,2,1,0:T(8,128)(2,1)S(1)}, u32[]{:S(2)}, u32[]{:S(2)}) async-start(bf16[4,4,256,256]{3,2,1,0:T(8,128)(2,1)} %maximum_bitcast_fusion), calls=%async_computation | async-start | bytes 4194304 | tf_op jit(solution)/shard_map/all_to_all | solution.py:179
  21.5 8.7 %add_select_fusion.1 = (s32[1792]{0:T(1024)S(1)}, s32[1792]{0:T(1024)S(1)}) fusion(s32[]{:T(128)S(6)} %mul.30, s32[]{:T(128)} %bitcast.38, s32[]{:T(128)} %bitcast.37, s32[]{:T(128)} %bitcast.36, s32[]{:T(128)} %bitcast.35, s32[]{:T(128)} %bitcast.34, s32[]{:T(128)} %bitcast.33, s32[]{:T(128)} %bitcast.32, s32[]{:T(128)} %bitcast.31, s32[]{:T(128)} %bitcast.30, ...), kind=kLoop, calls=%fused_computation.67 | loop fusion | flops 78848 | bytes 14396 | tf_op jit(solution)/shard_map/jit(floor_divide)/jit(_where)/select_n | solution.py:185
  31.0 9.5 %select_select_fusion.2 = (s32[1792]{0:T(1024)S(1)}, s32[1792]{0:T(1024)S(1)}) fusion(s32[]{:T(128)} %bitcast.22, s32[]{:T(128)} %bitcast.21, s32[]{:T(128)} %bitcast.20, s32[]{:T(128)} %bitcast.19, s32[]{:T(128)} %bitcast.18, s32[]{:T(128)} %bitcast.17, s32[]{:T(128)} %bitcast.16, s32[]{:T(128)} %bitcast.15, s32[]{:T(128)} %bitcast.14, s32[]{:T(128)} %bitcast.13, ...), kind=kLoop, calls=%fused_computation.73 | loop fusion | flops 82432 | bytes 14400 | tf_op jit(solution)/shard_map/jit(_where)/select_n | solution.py:189
  41.8 27.5 %all-to-all-done.x_ref = bf16[4,4,256,256]{3,2,1,0:T(8,128)(2,1)S(1)} async-done(((bf16[4,4,256,256]{3,2,1,0:T(8,128)(2,1)}), bf16[4,4,256,256]{3,2,1,0:T(8,128)(2,1)S(1)}, u32[]{:S(2)}, u32[]{:S(2)}) %all-to-all-start) | async-done | bytes 2097184 | tf_op jit(solution)/shard_map/all_to_all | solution.py:179
  69.4 1.5 collective-permute-start
  70.9 1.9 fusion.29
  72.7 22.3 %fusion.9.key_img = s32[1792,1]{1,0:T(8,128)S(1)} fusion(s32[]{:T(128)} %bitcast.38, s32[]{:T(128)} %bitcast.37, s32[]{:T(128)} %bitcast.36, s32[]{:T(128)} %bitcast.35, s32[]{:T(128)} %bitcast.34, s32[]{:T(128)} %bitcast.33, s32[]{:T(128)} %bitcast.32, s32[]{:T(128)} %bitcast.31, s32[]{:T(128)} %bitcast.30, s32[]{:T(128)} %bitcast.29, s32[]{:T(128)} %bitcast.28, ...), kind=kLoop, calls=%fused_computation.24 | loop fusion | flops 134400 | bytes 7300 | tf_op jit(solution)/shard_map/jit(_where)/select_n | solution.py:193
  95.1 9.5 %collective-permute-done.prev_ref = bf16[3,2,256,256]{3,2,1,0:T(8,128)(2,1)S(1)} collective-permute-done((bf16[3,2,256,256]{3,2,1,0:T(8,128)(2,1)S(1)}, bf16[3,2,256,256]{3,2,1,0:T(8,128)(2,1)S(1)}, u32[]{:S(2)}, u32[]{:S(2)}) %collective-permute-start) | collective-permute-done | bytes 786464 | tf_op jit(solution)/shard_map/ppermute | solution.py:34
  104.6 12.8 %shard_map.225 = (bf16[4,256,256]{2,1,0:T(8,128)(2,1)S(1)}, f32[4,2,256,256]{3,2,1,0:T(8,128)S(1)}, bf16[3,2,256,256]{3,2,1,0:T(8,128)(2,1)S(1)}) custom-call(bf16[4,4,256,256]{3,2,1,0:T(8,128)(2,1)S(1)} %all-to-all-done.x_ref, bf16[3,2,256,256]{3,2,1,0:T(8,128)(2,1)S(1)} %collective-permute-done.prev_ref, s32[1792,1]{1,0:T(8,128)S(1)} %copy-done.1, ...), custom_call_target="tpu_custom_call" | custom-call | flops 2852126720 | bytes 11010048 | tf_op jit(solution)/shard_map/pallas_call | solution.py:204
  117.3 1.5 collective-permute-start.1
  118.9 37.1 %collective-permute-done.1 = bf16[3,2,256,256]{3,2,1,0:T(8,128)(2,1)S(1)} collective-permute-done((bf16[3,2,256,256]{3,2,1,0:T(8,128)(2,1)S(1)}, bf16[3,2,256,256]{3,2,1,0:T(8,128)(2,1)S(1)}, u32[]{:S(2)}, u32[]{:S(2)}) %collective-permute-start.1) | collective-permute-done | bytes 786464 | tf_op jit(solution)/shard_map/ppermute | solution.py:34
  156.4 22.5 %all_to_all.10 = bf16[4,3,256,256]{3,2,1,0:T(8,128)(2,1)S(1)} all-to-all(bf16[4,3,256,256]{3,2,1,0:T(8,128)(2,1)S(1)} %maximum_maximum_fusion), channel_id=1, replica_groups={{0,1,2,3},{4,5,6,7},{8,9,10,11},{12,13,14,15},{16,17,18,19},{20,21,22,2..., dimensions={0} | all-to-all | bytes 3145728 | tf_op jit(solution)/shard_map/all_to_all | solution.py:244
  178.9 1.6 copy.82
  180.5 13.0 %fusion.1 = bf16[4096,256]{0,1:T(8,128)(2,1)} fusion(bf16[3,256,1024]{1,2,0:T(8,128)(2,1)} %bitcast.112, bf16[3,4096,1024]{2,1,0:T(8,128)(2,1)} %all-gather.2.cloned.1.call-done), kind=kOutput, calls=%fused_computation.2 | convolution fusion | flops 6443499520 | bytes 28835840 | tf_op jit(solution)/shard_map/prk,ptk->rt/dot_general | solution.py:524
  194.2 3.4 %collective-permute-start.2 = (bf16[2,1,1,8,128]{4,3,2,1,0:T(8,128)(2,1)S(1)}, bf16[2,1,1,8,128]{4,3,2,1,0:T(8,128)(2,1)S(1)}, u32[]{:S(2)}, u32[]{:S(2)}) collective-permute-start(bf16[2,1,1,8,128]{4,3,2,1,0:T(8,128)(2,1)S(1)} %get-tuple-element.55), channel_id=1, source_target_pairs={{0,16},{1,17},{2,18},{3,19},{4,20},{5,21},{6,22},{7,23},{8,24},{9,... | collective-permute-start | bytes 12296 | tf_op jit(solution)/shard_map/ppermute | solution.py:45
  197.6 1.3 collective-permute-start.3
  204.3 23.2 %reduce-scatter.2.cloned.1.call-done = bf16[2048,256]{0,1:T(8,128)(2,1)} async-done(((bf16[4096,256]{0,1:T(8,128)(2,1)}), bf16[2048,256]{0,1:T(8,128)(2,1)}) %reduce-scatter.2.cloned.1.call-update) | async-done | bytes 1048592 | tf_op jit(solution)/shard_map/reduce_scatter | solution.py:531
  227.5 1.7 fusion.38
  229.3 62.8 %shard_map.226 = (f32[72,128]{1,0:T(8,128)S(1)}, f32[72,256]{1,0:T(8,128)S(1)}, f32[72,128]{1,0:T(8,128)S(1)}, f32[72,256]{1,0:T(8,128)S(1)}, f32[72,128]{1,0:T(8,128)S(1)}, /*index=5*/f32[72,256]{1,0:T(8,128)S(1)}) custom-call(s32[16]{0:T(128)S(1)} %copy-done.9, f32[80,256]{1,0:T(8,128)S(1)} %pad.16.seg_ref, bf16[80,256]{1,0:T(8,128)(2,1)S(1)} %pad.17.klow_ref, ...), custom_call_target="tpu_custom_call" | custom-call | flops 1000000000 | bytes 4000000 | tf_op jit(solution)/shard_map/pallas_call | solution.py:472
  292.2 1.3 copy.86
  (81 shorter events, 13.2 us)
Async XLA Ops:
  7.2 220.4 %copy-start = (bf16[256,2048]{1,0:T(8,128)(2,1)S(1)}, bf16[256,2048]{1,0:T(8,128)(2,1)}, u32[]{:S(2)}) copy-start(bf16[256,2048]{1,0:T(8,128)(2,1)} %param.27) | copy-start | bytes 3145732
  7.2 2.2 copy-start.11
  7.2 173.3 %all-gather.2.cloned.1.call-start = ((), (), s32[]{:S(2)}) async-start(), calls=%async_computation.3 | async-start | bytes 26738688 | tf_op jit(solution)/shard_map/all_gather | solution.py:526
  16.2 4.4 %copy-start.15 = (s32[8]{0:T(128)S(1)}, s32[8]{0:T(128)}, u32[]{:S(2)}) copy-start(s32[8]{0:T(128)} %param.23) | copy-start | bytes 100
  16.2 4.6 %copy-start.14 = (s32[16]{0:T(128)S(1)}, s32[16]{0:T(128)}, u32[]{:S(2)}) copy-start(s32[16]{0:T(128)} %param.25) | copy-start | bytes 196
  16.2 14.1 %copy-start.13 = (s32[16]{0:T(128)S(1)}, s32[16]{0:T(128)}, u32[]{:S(2)}) copy-start(s32[16]{0:T(128)} %param.24) | copy-start | bytes 196
  16.2 53.1 %all-to-all-start = ((bf16[4,4,256,256]{3,2,1,0:T(8,128)(2,1)}), bf16[4,4,256,256]{3,2,1,0:T(8,128)(2,1)S(1)}, u32[]{:S(2)}, u32[]{:S(2)}) async-start(bf16[4,4,256,256]{3,2,1,0:T(8,128)(2,1)} %maximum_bitcast_fusion), calls=%async_computation | async-start | bytes 4194304 | tf_op jit(solution)/shard_map/all_to_all | solution.py:179
  20.6 206.9 %reduce-scatter.2.cloned.1.call-start = ((), (), s32[]{:S(2)}) async-start(), calls=%async_computation.4 | async-start | bytes 3145728 | tf_op jit(solution)/shard_map/reduce_scatter | solution.py:531
  69.3 35.2 %copy-start.1 = (s32[1792,1]{1,0:T(8,128)S(1)}, s32[1792,1]{1,0:T(8,128)}, u32[]{:S(2)}) copy-start(s32[1792,1]{1,0:T(8,128)} %reshape_select_fusion.key_doc) | copy-start | bytes 21508
  69.4 35.2 %collective-permute-start = (bf16[3,2,256,256]{3,2,1,0:T(8,128)(2,1)S(1)}, bf16[3,2,256,256]{3,2,1,0:T(8,128)(2,1)S(1)}, u32[]{:S(2)}, u32[]{:S(2)}) collective-permute-start(bf16[3,2,256,256]{3,2,1,0:T(8,128)(2,1)S(1)} %slice.203), channel_id=1, source_target_pairs={{0,4},{1,5},{2,6},{3,7},{4,8},{5,9},{6,10},{7,11},{8,12},{9,13},{1... | collective-permute-start | bytes 2359304 | tf_op jit(solution)/shard_map/ppermute | solution.py:34
  117.3 38.6 %collective-permute-start.1 = (bf16[3,2,256,256]{3,2,1,0:T(8,128)(2,1)S(1)}, bf16[3,2,256,256]{3,2,1,0:T(8,128)(2,1)S(1)}, u32[]{:S(2)}, u32[]{:S(2)}) collective-permute-start(bf16[3,2,256,256]{3,2,1,0:T(8,128)(2,1)S(1)} %get-tuple-element.18), channel_id=1, source_target_pairs={{4,0},{5,1},{6,2},{7,3},{8,4},{9,5},{10,6},{11,7},{12,8},{13,9},{1... | collective-permute-start | bytes 2359304 | tf_op jit(solution)/shard_map/ppermute | solution.py:34
  193.5 0.7 copy-start.3
  193.5 0.7 copy-start.12
  193.5 8.0 %copy-start.2 = (f32[72,256]{1,0:T(8,128)S(1)}, f32[72,256]{1,0:T(8,128)}, u32[]{:S(2)}) copy-start(f32[72,256]{1,0:T(8,128)} %kern2.1) | copy-start | bytes 221188
  194.2 8.0 %collective-permute-start.2 = (bf16[2,1,1,8,128]{4,3,2,1,0:T(8,128)(2,1)S(1)}, bf16[2,1,1,8,128]{4,3,2,1,0:T(8,128)(2,1)S(1)}, u32[]{:S(2)}, u32[]{:S(2)}) collective-permute-start(bf16[2,1,1,8,128]{4,3,2,1,0:T(8,128)(2,1)S(1)} %get-tuple-element.55), channel_id=1, source_target_pairs={{0,16},{1,17},{2,18},{3,19},{4,20},{5,21},{6,22},{7,23},{8,24},{9,... | collective-permute-start | bytes 12296 | tf_op jit(solution)/shard_map/ppermute | solution.py:45
  197.6 5.5 %collective-permute-start.3 = (bf16[2,1,1,8,128]{4,3,2,1,0:T(8,128)(2,1)S(1)}, bf16[2,1,1,8,128]{4,3,2,1,0:T(8,128)(2,1)S(1)}, u32[]{:S(2)}, u32[]{:S(2)}) collective-permute-start(bf16[2,1,1,8,128]{4,3,2,1,0:T(8,128)(2,1)S(1)} %get-tuple-element.56), channel_id=1, source_target_pairs={{16,0},{17,1},{18,2},{19,3},{20,4},{21,5},{22,6},{23,7},{24,8},{25... | collective-permute-start | bytes 12296 | tf_op jit(solution)/shard_map/ppermute | solution.py:47
  204.1 25.2 %copy-start.4 = (f32[72,256]{1,0:T(8,128)S(1)}, f32[72,256]{1,0:T(8,128)}, u32[]{:S(2)}) copy-start(f32[72,256]{1,0:T(8,128)} %mean2.1) | copy-start | bytes 221188
  204.1 25.2 %copy-start.5 = (f32[72,256]{1,0:T(8,128)S(1)}, f32[72,256]{1,0:T(8,128)}, u32[]{:S(2)}) copy-start(f32[72,256]{1,0:T(8,128)} %sq2.1) | copy-start | bytes 221188
  204.2 25.2 %copy-start.6 = (f32[72,128]{1,0:T(8,128)S(1)}, f32[72,128]{1,0:T(8,128)}, u32[]{:S(2)}) copy-start(f32[72,128]{1,0:T(8,128)} %kern1.1) | copy-start | bytes 110596
  204.2 25.2 %copy-start.7 = (f32[72,128]{1,0:T(8,128)S(1)}, f32[72,128]{1,0:T(8,128)}, u32[]{:S(2)}) copy-start(f32[72,128]{1,0:T(8,128)} %mean1.1) | copy-start | bytes 110596
  204.2 25.1 %copy-start.8 = (f32[72,128]{1,0:T(8,128)S(1)}, f32[72,128]{1,0:T(8,128)}, u32[]{:S(2)}) copy-start(f32[72,128]{1,0:T(8,128)} %sq1.1) | copy-start | bytes 110596
  204.2 25.1 %copy-start.9 = (s32[16]{0:T(128)S(1)}, s32[16]{0:T(128)}, u32[]{:S(2)}) copy-start(s32[16]{0:T(128)} %slab_ref.1) | copy-start | bytes 196
  229.2 62.9 %copy-start.10 = (bf16[2048,256]{0,1:T(8,128)(2,1)S(1)}, bf16[2048,256]{0,1:T(8,128)(2,1)}, u32[]{:S(2)}) copy-start(bf16[2048,256]{0,1:T(8,128)(2,1)} %reduce-scatter.2.cloned.1.call-done) | copy-start | bytes 3145732
Sparse Core Ops, SparseCore 0:
  9.6 161.1 all-gather.1
  193.7 33.8 reduce-scatter.1

commit v2 on v1

--- a/solution.py
+++ b/solution.py
@@ -191,7 +191,11 @@
     local = place - block * rows
     inside = (place >= 0) & (present > 0) & (local >= start) & (local < start + IMGTOK)
     image = jnp.where(inside, block, -1)
-    doc = jnp.where(place >= 0, doc_number(place, doc_lengths), -1)
+    ends = jnp.cumsum(doc_lengths)
+    doc = jnp.where(place >= 0, 0, -1)
+    for n in range(doc_lengths.shape[0]):
+        doc = doc + (place >= ends[n]).astype(jnp.int32)
+    doc, image = lax.optimization_barrier((doc, image))
     total = (front + reach) * rows
     heads = part // HD
 
@@ -521,17 +525,24 @@
     grads = (attend_heads if split else attend_ring)(
         queries, keys, values, out_grad, doc_lengths, image_count, image_offset
     )
-    partial_value = jnp.einsum(
-        "prk,ptk->rt",
-        lax.all_gather(qkv_weight, "wide", axis=1, tiled=True),
-        grads,
-        preferred_element_type=jnp.float32,
-    ).astype(jnp.bfloat16)
-    input_grad_t = (
-        lax.psum_scatter(partial_value, "head", scatter_dimension=0, tiled=True)
-        .astype(jnp.float32)
-        .astype(jnp.bfloat16)
-    )
+    weight = lax.all_gather(qkv_weight, "wide", axis=1, tiled=True)
+    if lax.axis_size("head") == 2:
+        half = weight.shape[1] // 2
+        head_index = lax.axis_index("head")
+
+        def features(owner):
+            rows = lax.dynamic_slice_in_dim(weight, owner * half, half, axis=1)
+            product = jnp.einsum("prk,ptk->rt", rows, grads, preferred_element_type=jnp.float32)
+            return product.astype(jnp.bfloat16)
+
+        arrived = lax.ppermute(features(1 - head_index), "head", [(0, 1), (1, 0)])
+        own = lax.optimization_barrier(features(head_index))
+        input_grad_t = (own.astype(jnp.float32) + arrived.astype(jnp.float32)).astype(jnp.bfloat16)
+    else:
+        partial_value = jnp.einsum(
+            "prk,ptk->rt", weight, grads, preferred_element_type=jnp.float32
+        ).astype(jnp.bfloat16)
+        input_grad_t = lax.psum_scatter(partial_value, "head", scatter_dimension=0, tiled=True)
     patch_part = lax.dot_general(
         input_grad_t, patch_weight, (((0,), (1,)), ((), ())), preferred_element_type=jnp.float32
     )

time: 305 us -> 299 us (0.980)
  blocking collectives: 22.5 us -> 52.6 us
  waiting for transfers between devices: 98.9 us -> 69.9 us
  other arithmetic: 47.8 us -> 30.8 us
  local copies, waits for them, and re-layouts: 15.4 us -> 20.4 us
    all_to_all x1, blocking collectives: 22.5 us -> 52.6 us  [attend_heads(): lax.all_to_all(packed, 'wide', split_axis=0, concat_axis=0, tiled=True, a...]
    reduce_scatter x1 -> x0, waiting for transfers between devices: 23.2 us -> none  [shards(): lax.psum_scatter(partial_value, 'head', scatter_dimension=0, tiled=True)]
    select_n x3 -> x0, other arithmetic: 19.4 us -> none  [the longest x1 9.47 us: attend_heads(): present = jnp.where(block == b, image_count[b], present)]
    ppermute x0 -> x1, waiting for transfers between devices: none -> 16.5 us  [shards(): arrived = lax.ppermute(features(1 - head_index), 'head', [(0, 1), (1, 0)])]
    ppermute x2, waiting for transfers between devices: 46.6 us -> 32.8 us  [passed_along(): return lax.ppermute(block, axis, route)]
    all_to_all x1, waiting for transfers between devices: 27.5 us -> 19 us  [attend_heads(): lax.all_to_all(grads, 'wide', split_axis=0, concat_axis=0, tiled=True, ax...]
    add x0 -> x1, other arithmetic: none -> 5.16 us  [attend_heads(): doc = doc + (place >= ends[n]).astype(jnp.int32)]
    select_n x2 -> x1, other arithmetic: 24.2 us -> 20 us  [attend_heads(): image = jnp.where(inside, block, -1)]
  transfers between devices with their start and end apart: 7 -> 7, of which waited for: 5 -> 5; matrix products, arithmetic and copies ran while one was open for 19% -> 17% of each run, Pallas kernels for 4% -> 5%
where the time goes in v2:
time: 299 us; the launch traced here: 298 us
  Pallas kernels  76.6 us (26%)
  waiting for transfers between devices  69.9 us (23%)
  blocking collectives  52.6 us (18%)
  other arithmetic  30.8 us (10%)
  local copies, waits for them, and re-layouts  20.4 us (7%)
  between operations  17.1 us (6%)
  matrix products  15.6 us (5%)
  starting transfers between devices  14.6 us (5%)
    pallas_call x1, Pallas kernels, conv_update(): pl.pallas_call(tail_kernel, in_specs=[pl.BlockSpec(memory_space=pltpu.SME...  62.6 us
    all_to_all x1, blocking collectives, attend_heads(): lax.all_to_all(packed, 'wide', split_axis=0, concat_axis=0, tiled=True, a...  52.6 us
    ppermute x2, waiting for transfers between devices, passed_along(): return lax.ppermute(block, axis, route)  32.8 us
    select_n x1, other arithmetic, attend_heads(): image = jnp.where(inside, block, -1)  20 us
    all_to_all x1, waiting for transfers between devices, attend_heads(): lax.all_to_all(grads, 'wide', split_axis=0, concat_axis=0, tiled=True, ax...  19 us
    ppermute x1, waiting for transfers between devices, shards(): arrived = lax.ppermute(features(1 - head_index), 'head', [(0, 1), (1, 0)])  16.5 us
    dot_general x2, matrix products, features(): jnp.einsum('prk,ptk->rt', rows, grads, preferred_element_type=jnp.float32)  15.1 us
    pallas_call x1, Pallas kernels, attend_heads(): pl.pallas_call(functools.partial(attend_kernel, reach), grid=(heads,), in...  14 us
  transfers between devices with their start and end apart: 7, of which 5 were waited for; matrix products, arithmetic and copies ran while one was open for 17% of the time, Pallas kernels for 5%

profile of v2, /device:TPU:0, one launch (start us, length us, event | category | flops | bytes accessed | tf_op | source)
XLA Modules:
  0.0 297.6 jit_solution(7377671171818803991)
XLA Ops:
  9.8 1.2 copy.61
  11.3 1.2 copy.62
  13.5 1.3 maximum_bitcast_fusion
  14.9 52.6 %all_to_all.10.x_ref = bf16[4,4,256,256]{3,2,1,0:T(8,128)(2,1)S(1)} all-to-all(bf16[4,4,256,256]{3,2,1,0:T(8,128)(2,1)S(1)} %maximum_bitcast_fusion), channel_id=1, replica_groups={{0,1,2,3},{4,5,6,7},{8,9,10,11},{12,13,14,15},{16,17,18,19},{20,21,22,2..., dimensions={0} | all-to-all | bytes 4194304 | tf_op jit(solution)/shard_map/all_to_all | solution.py:179
  68.4 2.3 collective-permute-start
  71.5 5.2 %convert_add_fusion = s32[1792]{0:T(1024)S(1)} fusion(s32[]{:T(128)} %bitcast.13, s32[]{:T(128)} %bitcast.12, s32[]{:T(128)} %bitcast.11, s32[]{:T(128)} %bitcast.10, s32[]{:T(128)} %bitcast.9, s32[]{:T(128)} %bitcast.8, s32[]{:T(128)} %bitcast.7, s32[]{:T(128)} %bitcast.6, s32[]{:T(128)S(6)} %mul.28), kind=kLoop, calls=%fused_computation.63 | loop fusion | flops 48384 | bytes 7204 | tf_op jit(solution)/shard_map/add | solution.py:197
  78.1 20.0 %fusion.43 = s32[1792]{0:T(1024)S(1)} fusion(s32[]{:T(128)} %bitcast.45, s32[]{:T(128)} %bitcast.44, s32[]{:T(128)} %bitcast.43, s32[]{:T(128)} %bitcast.42, s32[]{:T(128)} %bitcast.41, s32[]{:T(128)} %bitcast.40, s32[]{:T(128)} %bitcast.39, s32[]{:T(128)} %bitcast.38, s32[]{:T(128)} %bitcast.37, s32[]{:T(128)} %bitcast.36, s32[]{:T(128)} %bitcast.35, ...), kind=kLoop, calls=%fused_computation.79 | loop fusion | flops 134400 | bytes 7300 | tf_op jit(solution)/shard_map/jit(_where)/select_n | solution.py:193
  98.7 5.2 %collective-permute-done.prev_ref = bf16[3,2,256,256]{3,2,1,0:T(8,128)(2,1)} collective-permute-done((bf16[3,2,256,256]{3,2,1,0:T(8,128)(2,1)}, bf16[3,2,256,256]{3,2,1,0:T(8,128)(2,1)}, u32[]{:S(2)}, u32[]{:S(2)}) %collective-permute-start) | collective-permute-done | bytes 786464 | tf_op jit(solution)/shard_map/ppermute | solution.py:34
  104.0 14.0 %shard_map.225 = (bf16[4,256,256]{2,1,0:T(8,128)(2,1)S(1)}, f32[4,2,256,256]{3,2,1,0:T(8,128)S(1)}, bf16[3,2,256,256]{3,2,1,0:T(8,128)(2,1)}) custom-call(bf16[4,4,256,256]{3,2,1,0:T(8,128)(2,1)S(1)} %all_to_all.10.x_ref, bf16[3,2,256,256]{3,2,1,0:T(8,128)(2,1)} %collective-permute-done.prev_ref, s32[1792,1]{1,0:T(8,128)S(1)} %broadcast_in_dim.164.key_doc, ...), custom_call_target="tpu_custom_call" | custom-call | flops 2852126720 | bytes 11010048 | tf_op jit(solution)/shard_map/pallas_call | solution.py:208
  118.0 1.4 copy-done.1
  120.2 1.4 collective-permute-start.1
  121.6 3.4 %collective-permute-start.3 = (bf16[2,1,1,8,128]{4,3,2,1,0:T(8,128)(2,1)S(1)}, bf16[2,1,1,8,128]{4,3,2,1,0:T(8,128)(2,1)S(1)}, u32[]{:S(2)}, u32[]{:S(2)}) collective-permute-start(bf16[2,1,1,8,128]{4,3,2,1,0:T(8,128)(2,1)S(1)} %get-tuple-element.31), channel_id=1, source_target_pairs={{0,16},{1,17},{2,18},{3,19},{4,20},{5,21},{6,22},{7,23},{8,24},{9,... | collective-permute-start | bytes 12296 | tf_op jit(solution)/shard_map/ppermute | solution.py:45
  125.1 1.3 collective-permute-start.4
  131.7 27.6 %collective-permute-done.1 = bf16[3,2,256,256]{3,2,1,0:T(8,128)(2,1)} collective-permute-done((bf16[3,2,256,256]{3,2,1,0:T(8,128)(2,1)}, bf16[3,2,256,256]{3,2,1,0:T(8,128)(2,1)}, u32[]{:S(2)}, u32[]{:S(2)}) %collective-permute-start.1) | collective-permute-done | bytes 786464 | tf_op jit(solution)/shard_map/ppermute | solution.py:34
  159.3 1.8 add_convert_fusion.1
  161.2 1.3 maximum_maximum_fusion
  162.5 4.6 %all-to-all-start.1 = ((bf16[4,3,256,256]{3,2,1,0:T(8,128)(2,1)}), bf16[4,3,256,256]{3,2,1,0:T(8,128)(2,1)}, u32[]{:S(2)}, u32[]{:S(2)}) async-start(bf16[4,3,256,256]{3,2,1,0:T(8,128)(2,1)} %maximum_maximum_fusion), calls=%async_computation.1 | async-start | bytes 3145728 | tf_op jit(solution)/shard_map/all_to_all | solution.py:248
  168.0 19.0 %all-to-all-done.1 = bf16[4,3,256,256]{3,2,1,0:T(8,128)(2,1)} async-done(((bf16[4,3,256,256]{3,2,1,0:T(8,128)(2,1)}), bf16[4,3,256,256]{3,2,1,0:T(8,128)(2,1)}, u32[]{:S(2)}, u32[]{:S(2)}) %all-to-all-start.1) | async-done | bytes 1572896 | tf_op jit(solution)/shard_map/all_to_all | solution.py:248
  187.0 2.6 copy.69
  189.6 8.6 %fusion.10 = bf16[2048,256]{1,0:T(8,128)(2,1)S(1)} fusion(bf16[3,256,1024]{1,2,0:T(8,128)(2,1)} %bitcast.118, bf16[3,4096,1024]{2,1,0:T(8,128)(2,1)} %all-gather.2.cloned.1.call-done, s32[]{:T(128)S(6)} %select_n.168), kind=kOutput, calls=%fused_computation.6 | convolution fusion | flops 3221749760 | bytes 15204356 | tf_op jit(solution)/shard_map/prk,ptk->rt/dot_general | solution.py:535
  198.2 1.6 collective-permute-start.2
  199.9 6.6 %fusion.13 = bf16[2048,256]{1,0:T(8,128)(2,1)S(1)} fusion(bf16[3,256,1024]{1,2,0:T(8,128)(2,1)S(1)} %bitcast.119, bf16[3,4096,1024]{2,1,0:T(8,128)(2,1)} %all-gather.2.cloned.1.call-done, s32[]{:T(128)S(6)} %select_n.131), kind=kOutput, calls=%fused_computation.7 | convolution fusion | flops 3221749760 | bytes 15204356 | tf_op jit(solution)/shard_map/prk,ptk->rt/dot_general | solution.py:535
  206.5 16.5 %collective-permute-done.2 = bf16[2048,256]{1,0:T(8,128)(2,1)S(1)} collective-permute-done((bf16[2048,256]{1,0:T(8,128)(2,1)S(1)}, bf16[2048,256]{1,0:T(8,128)(2,1)S(1)}, u32[]{:S(2)}, u32[]{:S(2)}) %collective-permute-start.2) | collective-permute-done | bytes 1048608 | tf_op jit(solution)/shard_map/ppermute | solution.py:538
  224.4 62.6 %shard_map.226 = (f32[72,128]{1,0:T(8,128)S(1)}, f32[72,256]{1,0:T(8,128)S(1)}, f32[72,128]{1,0:T(8,128)S(1)}, f32[72,256]{1,0:T(8,128)S(1)}, f32[72,128]{1,0:T(8,128)S(1)}, /*index=5*/f32[72,256]{1,0:T(8,128)S(1)}) custom-call(s32[16]{0:T(128)S(1)} %copy-done.11, f32[80,256]{1,0:T(8,128)S(1)} %pad.16.seg_ref, bf16[80,256]{1,0:T(8,128)(2,1)S(1)} %pad.17.klow_ref, ...), custom_call_target="tpu_custom_call" | custom-call | flops 1000000000 | bytes 4000000 | tf_op jit(solution)/shard_map/pallas_call | solution.py:476
  (86 shorter events, 17.3 us)
Async XLA Ops:
  7.2 216.0 %copy-start = (bf16[256,2048]{1,0:T(8,128)(2,1)S(1)}, bf16[256,2048]{1,0:T(8,128)(2,1)}, u32[]{:S(2)}) copy-start(bf16[256,2048]{1,0:T(8,128)(2,1)} %param.27) | copy-start | bytes 3145732
  7.2 2.2 copy-start.14
  7.2 182.4 %all-gather.2.cloned.1.call-start = ((), (), s32[]{:S(2)}) async-start(), calls=%async_computation.2 | async-start | bytes 26738688 | tf_op jit(solution)/shard_map/all_gather | solution.py:528
  14.8 55.8 %copy-start.18 = (s32[8]{0:T(128)S(1)}, s32[8]{0:T(128)}, u32[]{:S(2)}) copy-start(s32[8]{0:T(128)} %param.23) | copy-start | bytes 100
  14.8 61.8 %copy-start.17 = (s32[16]{0:T(128)S(1)}, s32[16]{0:T(128)}, u32[]{:S(2)}) copy-start(s32[16]{0:T(128)} %param.24) | copy-start | bytes 196
  14.8 62.5 %copy-start.16 = (s32[16]{0:T(128)S(1)}, s32[16]{0:T(128)}, u32[]{:S(2)}) copy-start(s32[16]{0:T(128)} %param.25) | copy-start | bytes 196
  68.4 35.6 %collective-permute-start = (bf16[3,2,256,256]{3,2,1,0:T(8,128)(2,1)}, bf16[3,2,256,256]{3,2,1,0:T(8,128)(2,1)}, u32[]{:S(2)}, u32[]{:S(2)}) collective-permute-start(bf16[3,2,256,256]{3,2,1,0:T(8,128)(2,1)} %slice.243), channel_id=1, source_target_pairs={{0,4},{1,5},{2,6},{3,7},{4,8},{5,9},{6,10},{7,11},{8,12},{9,13},{1... | collective-permute-start | bytes 2359304 | tf_op jit(solution)/shard_map/ppermute | solution.py:34
  104.0 17.6 %copy-start.5 = (bf16[1,4,8,128]{3,2,1,0:T(8,128)(2,1)S(1)}, bf16[1,4,8,128]{3,2,1,0:T(8,128)(2,1)}, u32[]{:S(2)}) copy-start(bf16[1,4,8,128]{3,2,1,0:T(8,128)(2,1)} %param.29) | copy-start | bytes 24580
  104.0 17.7 %copy-start.15 = (bf16[1,4,8,128]{3,2,1,0:T(8,128)(2,1)S(1)}, bf16[1,4,8,128]{3,2,1,0:T(8,128)(2,1)}, u32[]{:S(2)}) copy-start(bf16[1,4,8,128]{3,2,1,0:T(8,128)(2,1)} %param.28) | copy-start | bytes 24580
  104.0 25.0 %copy-start.4 = (f32[72,256]{1,0:T(8,128)S(1)}, f32[72,256]{1,0:T(8,128)}, u32[]{:S(2)}) copy-start(f32[72,256]{1,0:T(8,128)} %kern2.1) | copy-start | bytes 221188
  118.0 1.4 copy-start.1
  120.2 41.0 %copy-start.3 = (bf16[4,256,256]{2,1,0:T(8,128)(2,1)S(1)}, bf16[4,256,256]{2,1,0:T(8,128)(2,1)}, u32[]{:S(2)}) copy-start(bf16[4,256,256]{2,1,0:T(8,128)(2,1)} %copy-done.2) | copy-start | bytes 1572868
  120.2 39.1 %collective-permute-start.1 = (bf16[3,2,256,256]{3,2,1,0:T(8,128)(2,1)}, bf16[3,2,256,256]{3,2,1,0:T(8,128)(2,1)}, u32[]{:S(2)}, u32[]{:S(2)}) collective-permute-start(bf16[3,2,256,256]{3,2,1,0:T(8,128)(2,1)} %get-tuple-element.22), channel_id=1, source_target_pairs={{4,0},{5,1},{6,2},{7,3},{8,4},{9,5},{10,6},{11,7},{12,8},{13,9},{1... | collective-permute-start | bytes 2359304 | tf_op jit(solution)/shard_map/ppermute | solution.py:34
  121.6 8.0 %collective-permute-start.3 = (bf16[2,1,1,8,128]{4,3,2,1,0:T(8,128)(2,1)S(1)}, bf16[2,1,1,8,128]{4,3,2,1,0:T(8,128)(2,1)S(1)}, u32[]{:S(2)}, u32[]{:S(2)}) collective-permute-start(bf16[2,1,1,8,128]{4,3,2,1,0:T(8,128)(2,1)S(1)} %get-tuple-element.31), channel_id=1, source_target_pairs={{0,16},{1,17},{2,18},{3,19},{4,20},{5,21},{6,22},{7,23},{8,24},{9,... | collective-permute-start | bytes 12296 | tf_op jit(solution)/shard_map/ppermute | solution.py:45
  125.1 5.5 %collective-permute-start.4 = (bf16[2,1,1,8,128]{4,3,2,1,0:T(8,128)(2,1)S(1)}, bf16[2,1,1,8,128]{4,3,2,1,0:T(8,128)(2,1)S(1)}, u32[]{:S(2)}, u32[]{:S(2)}) collective-permute-start(bf16[2,1,1,8,128]{4,3,2,1,0:T(8,128)(2,1)S(1)} %get-tuple-element.32), channel_id=1, source_target_pairs={{16,0},{17,1},{18,2},{19,3},{20,4},{21,5},{22,6},{23,7},{24,8},{25... | collective-permute-start | bytes 12296 | tf_op jit(solution)/shard_map/ppermute | solution.py:47
  162.5 24.5 %all-to-all-start.1 = ((bf16[4,3,256,256]{3,2,1,0:T(8,128)(2,1)}), bf16[4,3,256,256]{3,2,1,0:T(8,128)(2,1)}, u32[]{:S(2)}, u32[]{:S(2)}) async-start(bf16[4,3,256,256]{3,2,1,0:T(8,128)(2,1)} %maximum_maximum_fusion), calls=%async_computation.1 | async-start | bytes 3145728 | tf_op jit(solution)/shard_map/all_to_all | solution.py:248
  189.6 10.3 %copy-start.13 = (bf16[3,256,4,256]{1,3,2,0:T(8,128)(2,1)S(1)}, bf16[3,256,4,256]{1,3,2,0:T(8,128)(2,1)}, u32[]{:S(2)}) copy-start(bf16[3,256,4,256]{1,3,2,0:T(8,128)(2,1)} %copy.69) | copy-start | bytes 4718596
  198.2 24.8 %collective-permute-start.2 = (bf16[2048,256]{1,0:T(8,128)(2,1)S(1)}, bf16[2048,256]{1,0:T(8,128)(2,1)S(1)}, u32[]{:S(2)}, u32[]{:S(2)}) collective-permute-start(bf16[2048,256]{1,0:T(8,128)(2,1)S(1)} %fusion.10), channel_id=1, source_target_pairs={{0,16},{16,0},{1,17},{17,1},{2,18},{18,2},{3,19},{19,3},{4,20},{20... | collective-permute-start | bytes 3145736 | tf_op jit(solution)/shard_map/ppermute | solution.py:538
  223.2 63.8 %copy-start.12 = (bf16[2048,256]{1,0:T(8,128)(2,1)}, bf16[2048,256]{1,0:T(8,128)(2,1)S(1)}, u32[]{:S(2)}) copy-start(bf16[2048,256]{1,0:T(8,128)(2,1)S(1)} %add_convert_fusion) | copy-start | bytes 3145732
  223.2 1.1 copy-start.7
  223.3 1.1 copy-start.8
  223.3 1.1 copy-start.9
  223.3 1.1 copy-start.10
  223.3 1.1 copy-start.11
  (2 other events, 1.8 us)
Sparse Core Ops, SparseCore 0:
  9.6 161.9 all-gather.1
